TPU v7x, 32 devices: a whole 2x2x4 slice. The times are simulated.
32 devices in a mesh: seq: 8 (over y, x, core), grp: 4 (over z).
Axes of the slice: x: 2, y: 2, z: 4, core: 2. Of those that a mesh axis runs over, the one named last changes fastest.
Arguments:
- tokens: bfloat16 [3072, 768], P('seq'), may hold values from -6 to 6
- cotangent: bfloat16 [3072, 768], P('seq'), may hold values from -6 to 6
- entry_weight: bfloat16 [768, 2304], replicated, may hold values from -0.21875 to 0.21875
- exit_weight: bfloat16 [768, 768], replicated, may hold values from -3.5 to 3.5
- up_weight: bfloat16 [768, 3072], replicated, may hold values from -0.21875 to 0.21875
- down_weight: bfloat16 [3072, 768], replicated, may hold values from -0.109375 to 0.109375
- first_gain: float32 [768], replicated, may hold values from 0.5 to 1.5
- first_bias: float32 [768], replicated, may hold values from -3 to 3
- second_gain: float32 [768], replicated, may hold values from 0.5 to 1.5
- second_bias: float32 [768], replicated, may hold values from -3 to 3
- dilations: int32 [4], replicated, may hold values from 2 to 8, as said below
- offsets: int32 [4, 12], replicated, may hold values from 0 to 7, as said below
Outputs:
- output: bfloat16 [3072, 768], P('seq')
- token_grad: bfloat16 [3072, 768], P('seq')
- entry_grad: float32 [768, 2304], P('seq')
- exit_grad: float32 [768, 768], P('seq')
- up_grad: float32 [768, 3072], P('seq')
- down_grad: float32 [3072, 768], P('seq')
- first_gain_grad: float32 [768], P('seq')
- first_bias_grad: float32 [768], P('seq')
- second_gain_grad: float32 [768], P('seq')
- second_bias_grad: float32 [768], P('seq')
Inputs may be any that keep to these rules, and one draw needn't show every extreme that they name: `dilations`: every rate is one of 2, 3, 4, 6 and 8; some group has 2 and another 8. offsets[g, h] lies in 0 to dilations[g] - 1; in every group one head has offset 0 and another dilations[g] - 1.
All inputs are finite; a program needn't handle non-finite values.
Results may differ from a plain program's by a relative error of at most 0.013.
Values may be sent and summed in bfloat16 or wider, within the bound.
A program may use at most 320 MiB of HBM per device.

v0:
```python
from functools import partial

import jax
import jax.numpy as jnp
from jax import lax
from jax.sharding import PartitionSpec as P

RATE_MIN = 2
RATE_MAX = 8


EPS = 1e-05
PRECISE = lax.Precision.HIGHEST


def norm_forward(values, gain_vec, bias_vec):
    centered = values - jnp.mean(values, axis=1, keepdims=True)
    inverse = lax.rsqrt(jnp.mean(centered * centered, axis=1, keepdims=True) + EPS)
    plain = centered * inverse
    return (plain * gain_vec + bias_vec, plain, inverse)


def norm_backward(upstream, plain, inverse, gain_vec):
    scaled = upstream * gain_vec
    inner = (
        scaled
        - jnp.mean(scaled, axis=1, keepdims=True)
        - plain * jnp.mean(scaled * plain, axis=1, keepdims=True)
    )
    return (inverse * inner, jnp.sum(upstream * plain, axis=0), jnp.sum(upstream, axis=0))


def key_weights(query_sp, query_pos, key_block, first_row, geometry):
    local_len, capacity, dilation, segment, head_offs, score_scale = geometry
    key_count = key_block.shape[0]
    key_heads = key_block.reshape(key_count, query_sp.shape[1], query_sp.shape[2])
    scores = (
        jnp.einsum("ihd,jhd->hij", query_sp, key_heads, preferred_element_type=jnp.float32)
        * score_scale
    )
    key_index = first_row + jnp.arange(key_count, dtype=jnp.int32)
    source = key_index // capacity
    within = key_index - source * capacity
    key_pos = source[None, :] * local_len + head_offs[:, None] + dilation * within[None, :]
    key_live = within < local_len // dilation
    earlier = key_pos[:, None, :] <= query_pos[:, :, None]
    segment_match = key_pos[:, None, :] // segment == query_pos[:, :, None] // segment
    allowed = earlier & segment_match & key_live[None, None, :]
    return (jnp.where(allowed, jnp.exp(scores), 0.0), key_heads)


def forward_block(running, pieces, first_row, query_sp, query_pos, geometry):
    numerator, denominator = running
    key_block, value_block = pieces
    weights, key_heads = key_weights(query_sp, query_pos, key_block, first_row, geometry)
    value_heads = value_block.reshape(key_heads.shape)
    numerator = numerator + jnp.einsum(
        "hij,jhd->hid",
        weights.astype(jnp.bfloat16),
        value_heads,
        preferred_element_type=jnp.float32,
    )
    return (numerator, denominator + jnp.sum(weights, axis=2))


def blockwise(step_fn, running, pieces, first_row, block_rows):
    total_rows = pieces[0].shape[0]
    if total_rows > block_rows and total_rows % block_rows == 0:
        number = total_rows // block_rows
        stacked_first = pieces[0].reshape(number, block_rows, pieces[0].shape[1])
        stacked_second = pieces[1].reshape(number, block_rows, pieces[1].shape[1])
        block_starts = first_row + block_rows * jnp.arange(number, dtype=jnp.int32)

        def advance(state, items):
            return (step_fn(state, (items[0], items[1]), items[2]), None)

        running, _ = lax.scan(advance, running, (stacked_first, stacked_second, block_starts))
        return running
    return step_fn(running, pieces, first_row)


def backward_block(running, items, query_sp, query_pos, grad_sp, shift_sp, geometry):
    key_block, value_block, first_row = items
    score_scale = geometry[5]
    weights, key_heads = key_weights(query_sp, query_pos, key_block, first_row, geometry)
    key_count = key_block.shape[0]
    value_heads = value_block.reshape(key_heads.shape)
    pressure = jnp.einsum("ihd,jhd->hij", grad_sp, value_heads, preferred_element_type=jnp.float32)
    slopes = (weights * (pressure - shift_sp[:, :, None])).astype(jnp.bfloat16)
    running = (
        running
        + jnp.einsum("hij,jhd->ihd", slopes, key_heads, preferred_element_type=jnp.float32)
        * score_scale
    )
    grad_keys = (
        jnp.einsum("hij,ihd->jhd", slopes, query_sp, preferred_element_type=jnp.float32)
        * score_scale
    )
    grad_values = jnp.einsum(
        "hij,ihd->jhd", weights.astype(jnp.bfloat16), grad_sp, preferred_element_type=jnp.float32
    )
    return (running, (grad_keys.reshape(key_count, -1), grad_values.reshape(key_count, -1)))


def local_weights(query_heads, key_heads, score_scale):
    local_len = query_heads.shape[0]
    scores = (
        jnp.einsum("ihd,jhd->hij", query_heads, key_heads, preferred_element_type=jnp.float32)
        * score_scale
    )
    positions = jnp.arange(local_len, dtype=jnp.int32)
    causal = positions[:, None] >= positions[None, :]
    return jnp.where(causal[None], jnp.exp(scores), 0.0)


def on_device(
    tokens,
    cotangent,
    entry_weight,
    exit_weight,
    up_weight,
    down_weight,
    first_gain,
    first_bias,
    second_gain,
    second_bias,
    dilations,
    offsets,
):
    local_len, width_model = tokens.shape
    head_count = offsets.shape[1]
    head_size = width_model // head_count
    score_scale = head_size ** (-0.5)
    capacity = local_len // RATE_MIN
    group_idx = lax.axis_index("grp")
    seq_index = lax.axis_index("seq")
    seq_count = lax.axis_size("seq")
    dilation = lax.dynamic_index_in_dim(dilations, group_idx, 0, keepdims=False)
    head_offs = lax.dynamic_index_in_dim(offsets, group_idx, 0, keepdims=False)
    segment = local_len * seq_count * dilation // RATE_MAX
    step_ids = jnp.arange(capacity, dtype=jnp.int32)
    row_live = step_ids < local_len // dilation
    local_rows = jnp.minimum(head_offs[:, None] + dilation * step_ids[None, :], local_len - 1)
    query_pos = jnp.where(
        row_live[None, :],
        seq_index * local_len + head_offs[:, None] + dilation * step_ids[None, :],
        -1,
    )
    geometry = (local_len, capacity, dilation, segment, head_offs, score_scale)
    head_shape = (local_len, head_count, head_size)
    selector = local_rows[:, :, None] == jnp.arange(local_len, dtype=jnp.int32)[None, None, :]
    select_low = selector.astype(jnp.bfloat16)
    select_full = selector.astype(jnp.float32)

    def pick(array_in):
        return jnp.einsum(
            "hci,ihd->chd", select_low, array_in, preferred_element_type=jnp.float32
        ).astype(jnp.bfloat16)

    def place_back(sparse_in):
        return jnp.einsum("hci,chd->ihd", select_full, sparse_in, precision=PRECISE)

    inputs = tokens.astype(jnp.float32)
    normed_one, plain_one, inverse_one = norm_forward(inputs, first_gain, first_bias)
    normed_low = normed_one.astype(jnp.bfloat16)
    packed = jnp.dot(normed_low, entry_weight, preferred_element_type=jnp.float32).astype(
        jnp.bfloat16
    )
    query_heads = packed[:, :width_model].reshape(head_shape)
    key_heads = packed[:, width_model : 2 * width_model].reshape(head_shape)
    value_heads = packed[:, 2 * width_model :].reshape(head_shape)
    query_sp = pick(query_heads)
    key_sp = pick(key_heads).reshape(capacity, width_model)
    value_sp = pick(value_heads).reshape(capacity, width_model)
    empty_state = (
        jnp.zeros((head_count, capacity, head_size), jnp.float32),
        jnp.zeros((head_count, capacity), jnp.float32),
    )
    forward_step = partial(forward_block, query_sp=query_sp, query_pos=query_pos, geometry=geometry)
    numerator, denominator = blockwise(
        forward_step,
        empty_state,
        (
            lax.all_gather(key_sp, "seq", axis=0, tiled=True),
            lax.all_gather(value_sp, "seq", axis=0, tiled=True),
        ),
        jnp.int32(0),
        8 * capacity,
    )

    def local_part(query_in, key_in, value_in):
        weights = local_weights(query_in, key_in, score_scale)
        local_num = jnp.einsum(
            "hij,jhd->ihd",
            weights.astype(jnp.bfloat16),
            value_in,
            preferred_element_type=jnp.float32,
        )
        return (local_num, jnp.sum(weights, axis=2).T)

    def local_none(query_in, key_in, value_in):
        return (jnp.zeros(head_shape, jnp.float32), jnp.zeros((local_len, head_count), jnp.float32))

    local_num, local_den = lax.cond(
        group_idx == 0, local_part, local_none, query_heads, key_heads, value_heads
    )
    numerator_full = (
        jnp.einsum("hci,hcd->ihd", select_full, numerator, precision=PRECISE) + local_num
    )
    denominator_full = (
        jnp.einsum("hci,hc->ih", select_full, denominator, precision=PRECISE) + local_den
    )
    merged_num, merged_den = lax.psum(
        (numerator_full.reshape(local_len, width_model), denominator_full), "grp"
    )
    attention = merged_num.reshape(head_shape) / merged_den[:, :, None]
    mixed = attention.reshape(local_len, width_model).astype(jnp.bfloat16)
    middle = inputs + jnp.dot(mixed, exit_weight, preferred_element_type=jnp.float32)
    normed_two, plain_two, inverse_two = norm_forward(middle, second_gain, second_bias)
    normed_two_low = normed_two.astype(jnp.bfloat16)
    hidden = jnp.dot(normed_two_low, up_weight, preferred_element_type=jnp.float32)
    active = jax.nn.gelu(hidden, approximate=False).astype(jnp.bfloat16)
    output = (middle + jnp.dot(active, down_weight, preferred_element_type=jnp.float32)).astype(
        jnp.bfloat16
    )
    down_grad = jnp.dot(active.T, cotangent, preferred_element_type=jnp.float32)
    grad_active = jnp.dot(cotangent, down_weight.T, preferred_element_type=jnp.float32)
    _, gelu_pull = jax.vjp(partial(jax.nn.gelu, approximate=False), hidden)
    grad_hidden = gelu_pull(grad_active)[0].astype(jnp.bfloat16)
    up_grad = jnp.dot(normed_two_low.T, grad_hidden, preferred_element_type=jnp.float32)
    grad_normed_two = jnp.dot(grad_hidden, up_weight.T, preferred_element_type=jnp.float32)
    grad_plain_two, second_gain_grad, second_bias_grad = norm_backward(
        grad_normed_two, plain_two, inverse_two, second_gain
    )
    grad_middle = cotangent.astype(jnp.float32) + grad_plain_two
    grad_branch = grad_middle.astype(jnp.bfloat16)
    exit_grad = jnp.dot(mixed.T, grad_branch, preferred_element_type=jnp.float32)
    grad_mixed_low = lax.optimization_barrier(
        jnp.dot(grad_branch, exit_weight.T, preferred_element_type=jnp.float32).astype(jnp.bfloat16)
    )
    grad_mixed = grad_mixed_low.astype(jnp.float32).reshape(head_shape)
    grad_numer = (grad_mixed / merged_den[:, :, None]).astype(jnp.bfloat16)
    row_shift = jnp.sum(grad_mixed * attention, axis=2) / merged_den
    grad_sp = pick(grad_numer)
    shift_sp = jnp.einsum("hci,ih->hc", select_full, row_shift, precision=PRECISE)
    back_keys, back_values = (
        lax.all_gather(key_sp, "seq", axis=0, tiled=True),
        lax.all_gather(value_sp, "seq", axis=0, tiled=True),
    )
    block_rows = 8 * capacity
    number = back_keys.shape[0] // block_rows
    stacked_keys = back_keys.reshape(number, block_rows, width_model)
    stacked_values = back_values.reshape(number, block_rows, width_model)
    block_starts = block_rows * jnp.arange(number, dtype=jnp.int32)
    empty_query = jnp.zeros((capacity, head_count, head_size), jnp.float32)
    back_step = partial(
        backward_block,
        query_sp=query_sp,
        query_pos=query_pos,
        grad_sp=grad_sp,
        shift_sp=shift_sp,
        geometry=geometry,
    )
    grad_query_sp, (grad_key_all, grad_value_all) = lax.scan(
        back_step, empty_query, (stacked_keys, stacked_values, block_starts)
    )
    own_keys, own_values = (
        lax.psum_scatter(
            grad_key_all.reshape(-1, width_model), "seq", scatter_dimension=0, tiled=True
        ),
        lax.psum_scatter(
            grad_value_all.reshape(-1, width_model), "seq", scatter_dimension=0, tiled=True
        ),
    )

    def local_grads(query_in, key_in, value_in, grad_in, shift_in):
        weights = local_weights(query_in, key_in, score_scale)
        pressure = jnp.einsum("ihd,jhd->hij", grad_in, value_in, preferred_element_type=jnp.float32)
        slopes = (weights * (pressure - shift_in.T[:, :, None])).astype(jnp.bfloat16)
        grad_query = (
            jnp.einsum("hij,jhd->ihd", slopes, key_in, preferred_element_type=jnp.float32)
            * score_scale
        )
        grad_key = (
            jnp.einsum("hij,ihd->jhd", slopes, query_in, preferred_element_type=jnp.float32)
            * score_scale
        )
        grad_value = jnp.einsum(
            "hij,ihd->jhd",
            weights.astype(jnp.bfloat16),
            grad_in,
            preferred_element_type=jnp.float32,
        )
        return (grad_query, grad_key, grad_value)

    def local_skip(query_in, key_in, value_in, grad_in, shift_in):
        zeros_heads = jnp.zeros(head_shape, jnp.float32)
        return (zeros_heads, zeros_heads, zeros_heads)

    local_dq, local_dk, local_dv = lax.cond(
        group_idx == 0,
        local_grads,
        local_skip,
        query_heads,
        key_heads,
        value_heads,
        grad_numer,
        row_shift,
    )
    grad_query_full = place_back(grad_query_sp) + local_dq
    grad_key_full = place_back(own_keys.reshape(capacity, head_count, head_size)) + local_dk
    grad_value_full = place_back(own_values.reshape(capacity, head_count, head_size)) + local_dv
    grad_packed = jnp.concatenate(
        [
            grad_query_full.reshape(local_len, width_model),
            grad_key_full.reshape(local_len, width_model),
            grad_value_full.reshape(local_len, width_model),
        ],
        axis=1,
    )
    summed = lax.psum(grad_packed, "grp").astype(jnp.bfloat16)
    entry_grad = jnp.dot(normed_low.T, summed, preferred_element_type=jnp.float32)
    grad_normed_one = jnp.dot(summed, entry_weight.T, preferred_element_type=jnp.float32)
    grad_plain_one, first_gain_grad, first_bias_grad = norm_backward(
        grad_normed_one, plain_one, inverse_one, first_gain
    )
    token_grad = (grad_middle + grad_plain_one).astype(jnp.bfloat16)
    shards = (
        lax.psum_scatter(entry_grad, "seq", scatter_dimension=0, tiled=True),
        lax.psum_scatter(exit_grad, "seq", scatter_dimension=0, tiled=True),
        lax.psum_scatter(up_grad, "seq", scatter_dimension=0, tiled=True),
        lax.psum_scatter(down_grad, "seq", scatter_dimension=0, tiled=True),
        lax.psum_scatter(first_gain_grad, "seq", scatter_dimension=0, tiled=True),
        lax.psum_scatter(first_bias_grad, "seq", scatter_dimension=0, tiled=True),
        lax.psum_scatter(second_gain_grad, "seq", scatter_dimension=0, tiled=True),
        lax.psum_scatter(second_bias_grad, "seq", scatter_dimension=0, tiled=True),
    )
    return (
        output,
        token_grad,
        shards[0],
        shards[1],
        shards[2],
        shards[3],
        shards[4],
        shards[5],
        shards[6],
        shards[7],
    )


def solution(mesh):
    return jax.shard_map(
        on_device,
        mesh=mesh,
        in_specs=(P("seq", None), P("seq", None), P(), P(), P(), P(), P(), P(), P(), P(), P(), P()),
        out_specs=(
            P("seq", None),
            P("seq", None),
            P("seq", None),
            P("seq", None),
            P("seq", None),
            P("seq", None),
            P("seq"),
            P("seq"),
            P("seq"),
            P("seq"),
        ),
        check_vma=False,
    )
```

profile of v0, /device:TPU:0, one launch (start us, length us, event | category | flops | bytes accessed | tf_op | source)
XLA Modules:
  0.0 617.6 jit_solution(17869681882909682034)
XLA Ops:
  38.2 6.6 %conditional.2 = (f32[384,12,64]{0,2,1:T(8,128)}, f32[384,12]{0,1:T(8,128)}) conditional(s32[]{:T(128)} %convert_element_type.101, () %tuple.26, (bf16[384,12,64]{0,2,1:T(8,128)(2,1)}, bf16[384,12,64]{0,2,1:T(8,128)(2,1)}, bf16[384,12,64]{0,2,1:T(8,128)(2,1)}) %tuple.79), branch_computations={%region_2.3_spmd, %region_3.5_spmd} | conditional | flops 463744512 | bytes 19925036 | solution.py:204
  38.3 3.8 fusion
  51.3 9.7 %all-gather.3.cloned.1.call-done = bf16[1536,768]{1,0:T(8,128)(2,1)} async-done(((bf16[192,768]{1,0:T(8,128)(2,1)}), bf16[1536,768]{1,0:T(8,128)(2,1)}) %all-gather.3.cloned.1.call-update) | async-done | bytes 2359312 | tf_op jit(solution)/shard_map/all_gather | solution.py:184
  61.1 4.3 copy.43
  65.3 11.3 %fusion.109 = (f32[12,192]{1,0:T(8,128)}, f32[12,192,1536]{2,1,0:T(8,128)}) fusion(bf16[192,12,64]{0,2,1:T(8,128)(2,1)} %fusion.76, bf16[1536,12,64]{0,2,1:T(8,128)(2,1)} %bitcast.129, pred[1536]{0:T(1024)(128)(4,1)} %fusion.101, s32[12,192]{1,0:T(8,128)} %get-tuple-element.117, s32[12,1536]{1,0:T(8,128)} %get-tuple-element.115, ...), kind=kOutput, calls=%fused_computation.170 | convolution fusion | flops 477755136 | bytes 16986624 | tf_op jit(solution)/shard_map/ihd,jhd->hij/dot_general | solution.py:38
  76.6 16.0 %all-gather.5.cloned.1.call-done = bf16[1536,768]{1,0:T(8,128)(2,1)} async-done(((bf16[192,768]{1,0:T(8,128)(2,1)}), bf16[1536,768]{1,0:T(8,128)(2,1)}) %all-gather.5.cloned.1.call-update) | async-done | bytes 2359312 | tf_op jit(solution)/shard_map/all_gather | solution.py:185
  92.6 4.3 copy.46
  96.8 8.1 %fusion.33 = f32[12,192,64]{1,2,0:T(8,128)S(1)} fusion(bf16[1536,12,64]{0,2,1:T(8,128)(2,1)} %bitcast.126, f32[12,192,1536]{2,1,0:T(8,128)} %get-tuple-element.120), kind=kOutput, calls=%fused_computation.50 | convolution fusion | flops 456523776 | bytes 17104896 | tf_op jit(solution)/shard_map/hij,jhd->hid/dot_general | solution.py:57
  104.9 3.8 fusion.62
  112.2 21.8 %psum.22 = f32[384,12]{0,1:T(8,128)} all-reduce(f32[384,12]{0,1:T(8,128)} %bitcast_add_fusion), channel_id=1, replica_groups=mesh['seq'=8,'grp'=4] {'grp'}, use_global_device_ids=true, to_apply=%region_7.8 | all-reduce | flops 4608 | bytes 36864 | tf_op jit(solution)/shard_map/psum | solution.py:213
  134.1 31.8 %all-reduce.8.cloned.1.call-done = f32[384,768]{0,1:T(8,128)} async-done(((f32[384,768]{0,1:T(8,128)}), f32[384,768]{0,1:T(8,128)}) %all-reduce.8.cloned.1.call-update) | async-done | bytes 1179664 | tf_op jit(solution)/shard_map/psum | solution.py:213
  170.7 4.6 fusion.106
  175.4 14.1 %add_convert_fusion = (bf16[384,3072]{1,0:T(8,128)(2,1)S(1)}, f32[384,3072]{1,0:T(8,128)}) fusion(f32[384,3072]{1,0:T(8,128)S(1)} %fusion.106, bf16[384,768]{1,0:T(8,128)(2,1)S(1)} %copy-done.18, bf16[3072,768]{1,0:T(8,128)(2,1)S(1)} %bitcast.156), kind=kOutput, calls=%fused_computation.30 | convolution fusion | flops 1896873984 | bytes 17104896 | tf_op jit(solution)/shard_map/dot_general | solution.py:227
  204.1 6.4 %multiply_convert_fusion.1 = bf16[12,192,1536]{2,1,0:T(8,128)(2,1)S(1)} fusion(f32[12,192,1536]{2,1,0:T(8,128)} %get-tuple-element.120, bf16[192,12,64]{0,2,1:T(8,128)(2,1)S(1)} %fusion.75, bf16[1536,12,64]{0,2,1:T(8,128)(2,1)S(1)} %bitcast.127, f32[12,192]{1,0:T(8,128)S(1)} %bitcast.150), kind=kOutput, calls=%fused_computation.26 | convolution fusion | flops 463601664 | bytes 23897088 | tf_op jit(solution)/shard_map/while/body/eval_jaxpr/ihd,jhd->hij/dot_general | solution.py:88
  210.6 4.1 convolution_multiply_fusion.2
  214.9 6.1 copy.53
  221.3 9.1 %fusion.31 = f32[12,64,1536]{2,1,0:T(8,128)} fusion(bf16[192,12,64]{0,2,1:T(8,128)(2,1)} %copy-done.25, f32[12,192,1536]{2,1,0:T(8,128)} %get-tuple-element.120), kind=kOutput, calls=%fused_computation.48 | convolution fusion | flops 456523776 | bytes 19169280 | tf_op jit(solution)/shard_map/while/body/eval_jaxpr/hij,ihd->jhd/dot_general | solution.py:99
  230.3 6.4 %copy.55 = f32[1536,768]{1,0:T(8,128)} copy(f32[1536,768]{0,1:T(8,128)} %bitcast.128) | data formatting | bytes 9437184
  236.8 3.7 fusion.91
  240.5 8.5 %fusion.105 = f32[768,3072]{1,0:T(8,128)} fusion(bf16[384,3072]{1,0:T(8,128)(2,1)} %copy-done.24, f32[384,768]{1,0:T(8,128)} %copy-done.3, f32[768]{0:T(1024)} %param.25, f32[768]{0:T(1024)} %param.24, f32[384]{0:T(512)} %copy-done.34, f32[384]{0:T(512)} %copy-done.30), kind=kOutput, calls=%fused_computation.167 | convolution fusion | flops 1813413888 | bytes 12985344 | tf_op jit(solution)/shard_map/dot_general | solution.py:230
  249.1 5.0 multiply_convert_fusion.2
  255.5 5.1 fusion.112
  260.7 9.4 %conditional.3 = (f32[384,12,64]{0,2,1:T(8,128)S(1)}, f32[384,12,64]{0,2,1:T(8,128)S(1)}, f32[384,12,64]{0,2,1:T(8,128)S(1)}) conditional(s32[]{:T(128)} %convert_element_type.101, () %tuple.28, (bf16[384,12,64]{0,2,1:T(8,128)(2,1)}, bf16[384,12,64]{0,2,1:T(8,128)(2,1)}, bf16[384,12,64]{0,2,1:T(8,128)(2,1)}, bf16[384,12,64]{0,2,1:T(8,128)(2,1)}, ...), branch_computations={%region_13.14_spmd, %region_14.15_spmd} | conditional | flops 1147355136 | bytes 49490084 | solution.py:300
  270.1 7.0 %fusion.70 = f32[192,12,64]{0,2,1:T(8,128)S(1)} fusion(bf16[1536,12,64]{0,2,1:T(8,128)(2,1)} %bitcast.130, bf16[12,192,1536]{2,1,0:T(8,128)(2,1)} %copy-done.1), kind=kOutput, calls=%fused_computation.94 | convolution fusion | flops 453132288 | bytes 10027008 | tf_op jit(solution)/shard_map/while/body/eval_jaxpr/hij,jhd->ihd/dot_general | solution.py:92
  282.1 50.1 %reduce-scatter.21.cloned.1.call-done = f32[192,768]{1,0:T(8,128)} async-done(((f32[1536,768]{1,0:T(8,128)}), f32[192,768]{1,0:T(8,128)}) %reduce-scatter.21.cloned.1.call-update) | async-done | bytes 589840
  341.9 126.0 %all-reduce.9 = bf16[384,2304]{0,1:T(8,128)(2,1)} all-reduce(f32[384,2304]{0,1:T(8,128)} %pad_maximum_fusion), channel_id=1, replica_groups=mesh['seq'=8,'grp'=4] {'grp'}, use_global_device_ids=true, to_apply=%region_17.18 | all-reduce | flops 884736 | bytes 5308416 | tf_op jit(solution)/shard_map/psum | solution.py:321
  467.9 8.2 %fusion.87 = f32[768,2304]{1,0:T(8,128)} fusion(bf16[384,2304]{0,1:T(8,128)(2,1)} %all-reduce.9, bf16[384,768]{1,0:T(8,128)(2,1)} %param.16, f32[768]{0:T(1024)S(1)} %copy-done.31, f32[768]{0:T(1024)S(1)} %copy-done.29, f32[384]{0:T(512)S(1)} %copy-done.36, f32[384]{0:T(512)S(1)} %copy-done.33), kind=kOutput, calls=%fused_computation.122 | convolution fusion | flops 1360723968 | bytes 9446400 | tf_op jit(solution)/shard_map/dot_general | solution.py:322
  478.0 7.2 %fusion.69 = bf16[384,768]{1,0:T(8,128)(2,1)} fusion(f32[384,768]{1,0:T(8,128)} %copy-done.3, bf16[384,3072]{1,0:T(8,128)(2,1)} %copy-done.6, bf16[3072,768]{1,0:T(8,128)(2,1)} %param.21), kind=kOutput, calls=%fused_computation.91 | convolution fusion | flops 1812529152 | bytes 8847360 | tf_op jit(solution)/shard_map/dot_general | solution.py:223
  485.2 3.6 fusion.84
  488.7 24.2 %all-reduce.4 = (f32[768]{0:T(1024)}, f32[768]{0:T(1024)}, f32[768]{0:T(1024)}, f32[768]{0:T(1024)}) all-reduce(f32[768]{0:T(1024)} %get-tuple-element.93, f32[768]{0:T(1024)} %get-tuple-element.98, f32[768]{0:T(1024)S(1)} %copy-done.40, f32[768]{0:T(1024)} %get-tuple-element.97), channel_id=8, replica_groups=mesh['seq'=8,'grp'=4] {'seq'}, use_global_device_ids=true, to_apply=%region_25.26.clone | all-reduce | flops 3072 | bytes 24576
  522.5 18.4 %reduce-scatter.17.cloned.1.call-done = f32[384,768]{1,0:T(8,128)} async-done(((f32[3072,768]{1,0:T(8,128)}), f32[384,768]{1,0:T(8,128)}) %reduce-scatter.17.cloned.1.call-update) | async-done | bytes 1179664 | tf_op jit(solution)/shard_map/reduce_scatter | solution.py:332
  540.8 70.0 %reduce-scatter.11.cloned.1.call-done = f32[96,2304]{1,0:T(8,128)} async-done(((f32[768,2304]{1,0:T(8,128)}), f32[96,2304]{1,0:T(8,128)}) %reduce-scatter.11.cloned.1.call-update) | async-done | bytes 884752 | tf_op jit(solution)/shard_map/reduce_scatter | solution.py:329
  (177 shorter events, 96.4 us)
Async XLA Ops:
  7.2 8.4 %copy-start = (bf16[768,2304]{1,0:T(8,128)(2,1)S(1)}, bf16[768,2304]{1,0:T(8,128)(2,1)}, u32[]{:S(2)}) copy-start(bf16[768,2304]{1,0:T(8,128)(2,1)} %param.18) | copy-start | bytes 10616836
  7.2 53.9 %all-gather.3.cloned.1.call-start = ((), (), s32[]{:S(2)}) async-start(), calls=%async_computation.6 | async-start | bytes 2654208 | tf_op jit(solution)/shard_map/all_gather | solution.py:184
  29.2 63.4 %all-gather.5.cloned.1.call-start = ((), (), s32[]{:S(2)}) async-start(), calls=%async_computation.7 | async-start | bytes 2654208 | tf_op jit(solution)/shard_map/all_gather | solution.py:185
  36.1 129.8 %all-reduce.8.cloned.1.call-start = ((), (), s32[]{:S(2)}) async-start(), calls=%async_computation.8 | async-start | bytes 2359296 | tf_op jit(solution)/shard_map/psum | solution.py:213
  108.7 171.1 %reduce-scatter.19.cloned.1.call-start = ((), (), s32[]{:S(2)}) async-start(), calls=%async_computation.13 | async-start | bytes 5308416
  165.9 4.8 copy-start.27
  165.9 4.8 copy-start.28
  168.1 7.3 %slice-start.2 = ((s8[4718592]{0:T(1024)(128)(4,1)}), s8[4194304]{0:T(1024)(128)(4,1)S(1)}, s32[]{:S(2)}) async-start(s8[4718592]{0:T(1024)(128)(4,1)} %bitcast.155), calls=%async_computation.17 | async-start | bytes 8388608
  170.4 22.0 %copy-start.3 = (f32[384,768]{1,0:T(8,128)}, f32[384,768]{1,0:T(8,128)S(1)}, u32[]{:S(2)}) copy-start(f32[384,768]{1,0:T(8,128)S(1)} %get-tuple-element.122) | copy-start | bytes 3538948
  170.4 22.0 %copy-start.30 = (f32[384]{0:T(512)}, f32[384]{0:T(512)S(1)}, u32[]{:S(2)}) copy-start(f32[384]{0:T(512)S(1)} %broadcast_multiply_fusion.5) | copy-start | bytes 4612
  170.7 21.7 %copy-start.34 = (f32[384]{0:T(512)}, f32[384]{0:T(512)S(1)}, u32[]{:S(2)}) copy-start(f32[384]{0:T(512)S(1)} %add_rsqrt_fusion) | copy-start | bytes 4612
  170.7 18.8 %slice-start = ((s8[4718592]{0:T(1024)(128)(4,1)}), s8[4194304]{0:T(1024)(128)(4,1)S(1)}, s32[]{:S(2)}) async-start(s8[4718592]{0:T(1024)(128)(4,1)} %bitcast.153), calls=%async_computation.15 | async-start | bytes 8388608
  175.4 14.1 %copy-start.16 = (f32[384,3072]{1,0:T(8,128)}, f32[384,3072]{1,0:T(8,128)S(1)}, u32[]{:S(2)}) copy-start(f32[384,3072]{1,0:T(8,128)S(1)} %fusion.106) | copy-start | bytes 14155780
  175.4 14.1 %slice-start.1 = ((s8[4718592]{0:T(1024)(128)(4,1)}), s8[524288]{0:T(1024)(128)(4,1)S(1)}, s32[]{:S(2)}) async-start(s8[4718592]{0:T(1024)(128)(4,1)} %bitcast.153), calls=%async_computation.16 | async-start | bytes 1048576
  197.7 6.4 %copy-start.2 = (bf16[1536,768]{0,1:T(8,128)(2,1)S(1)}, bf16[1536,768]{0,1:T(8,128)(2,1)}, u32[]{:S(2)}) copy-start(bf16[1536,768]{0,1:T(8,128)(2,1)} %copy.46) | copy-start | bytes 7077892
  204.1 6.4 %copy-start.25 = (bf16[192,12,64]{0,2,1:T(8,128)(2,1)}, bf16[192,12,64]{0,2,1:T(8,128)(2,1)S(1)}, u32[]{:S(2)}) copy-start(bf16[192,12,64]{0,2,1:T(8,128)(2,1)S(1)} %fusion.75) | copy-start | bytes 884740
  204.1 6.4 %copy-start.26 = (bf16[192,12,64]{0,2,1:T(8,128)(2,1)S(1)}, bf16[192,12,64]{0,2,1:T(8,128)(2,1)}, u32[]{:S(2)}) copy-start(bf16[192,12,64]{0,2,1:T(8,128)(2,1)} %fusion.76) | copy-start | bytes 884740
  221.0 111.2 %reduce-scatter.21.cloned.1.call-start = ((), (), s32[]{:S(2)}) async-start(), calls=%async_computation.14 | async-start | bytes 5308416
  236.7 285.7 %reduce-scatter.13.cloned.1.call-start = ((), (), s32[]{:S(2)}) async-start(), calls=%async_computation.10 | async-start | bytes 2654208 | tf_op jit(solution)/shard_map/reduce_scatter | solution.py:330
  240.5 282.0 %reduce-scatter.15.cloned.1.call-start = ((), (), s32[]{:S(2)}) async-start(), calls=%async_computation.11 | async-start | bytes 10616832 | tf_op jit(solution)/shard_map/reduce_scatter | solution.py:331
  249.1 291.8 %reduce-scatter.17.cloned.1.call-start = ((), (), s32[]{:S(2)}) async-start(), calls=%async_computation.12 | async-start | bytes 10616832 | tf_op jit(solution)/shard_map/reduce_scatter | solution.py:332
  249.1 6.4 %copy-start.19 = (bf16[384,768]{1,0:T(8,128)(2,1)S(1)}, bf16[384,768]{1,0:T(8,128)(2,1)}, u32[]{:S(2)}) copy-start(bf16[384,768]{1,0:T(8,128)(2,1)} %param.17) | copy-start | bytes 1769476
  260.7 350.2 %reduce-scatter.11.cloned.1.call-start = ((), (), s32[]{:S(2)}) async-start(), calls=%async_computation.9 | async-start | bytes 7962624 | tf_op jit(solution)/shard_map/reduce_scatter | solution.py:329
  270.1 7.0 %copy-start.12 = (f32[384,12,64]{0,2,1:T(8,128)}, f32[384,12,64]{0,2,1:T(8,128)S(1)}, u32[]{:S(2)}) copy-start(f32[384,12,64]{0,2,1:T(8,128)S(1)} %get-tuple-element.82) | copy-start | bytes 3538948
  270.1 7.0 %copy-start.14 = (f32[384,12,64]{0,2,1:T(8,128)}, f32[384,12,64]{0,2,1:T(8,128)S(1)}, u32[]{:S(2)}) copy-start(f32[384,12,64]{0,2,1:T(8,128)S(1)} %get-tuple-element.81) | copy-start | bytes 3538948
  334.4 5.4 copy-start.11
  341.9 126.0 %copy-start.29 = (f32[768]{0:T(1024)S(1)}, f32[768]{0:T(1024)}, u32[]{:S(2)}) copy-start(f32[768]{0:T(1024)} %param.22) | copy-start | bytes 9220
  341.9 126.0 %copy-start.31 = (f32[768]{0:T(1024)S(1)}, f32[768]{0:T(1024)}, u32[]{:S(2)}) copy-start(f32[768]{0:T(1024)} %param.23) | copy-start | bytes 9220
  341.9 126.0 %copy-start.33 = (f32[384]{0:T(512)S(1)}, f32[384]{0:T(512)}, u32[]{:S(2)}) copy-start(f32[384]{0:T(512)} %copy-done.32) | copy-start | bytes 4612
  341.9 126.0 %copy-start.36 = (f32[384]{0:T(512)S(1)}, f32[384]{0:T(512)}, u32[]{:S(2)}) copy-start(f32[384]{0:T(512)} %copy-done.35) | copy-start | bytes 4612
  478.0 7.2 %copy-start.5 = (bf16[384,768]{1,0:T(8,128)(2,1)S(1)}, bf16[384,768]{1,0:T(8,128)(2,1)}, u32[]{:S(2)}) copy-start(bf16[384,768]{1,0:T(8,128)(2,1)} %param.16) | copy-start | bytes 1769476
  478.0 7.2 %copy-start.7 = (bf16[384,2304]{0,1:T(8,128)(2,1)S(1)}, bf16[384,2304]{0,1:T(8,128)(2,1)}, u32[]{:S(2)}) copy-start(bf16[384,2304]{0,1:T(8,128)(2,1)} %all-reduce.9) | copy-start | bytes 5308420
  (23 other events, 59.1 us)
Sparse Core Ops, SparseCore 0:
  29.3 31.7 all-gather.2
  63.5 29.0 all-gather.4
  108.9 56.9 all-reduce.7
  221.1 53.4 reduce-scatter.18
  278.3 53.8 reduce-scatter.20
  336.0 42.4 reduce-scatter.12
  382.9 76.4 reduce-scatter.14
  463.9 76.8 reduce-scatter.16
  545.3 65.4 reduce-scatter.10
where the time goes:
time: 626 us; the launch traced here: 618 us
  waiting for transfers between devices  196 us (31%)
  blocking collectives  172 us (27%)
  matrix products  151 us (24%)
  local copies, waits for them, and re-layouts  51.3 us (8%)
  other arithmetic  28 us (4%)
  between operations  17.8 us (3%)
    psum x1, blocking collectives, on_device(): summed = lax.psum(grad_packed, 'grp').astype(jnp.bfloat16)  126 us
    reduce_scatter x1, waiting for transfers between devices, on_device(): lax.psum_scatter(entry_grad, 'seq', scatter_dimension=0, tiled=True)  70 us
    unnamed x11, waiting for transfers between devices  50.2 us
    psum x1, waiting for transfers between devices, on_device(): lax.psum((numerator_full.reshape(local_len, width_model), denominator_ful...  31.8 us
    unnamed x89, local copies, waits for them, and re-layouts  27.3 us
    unnamed x1, blocking collectives  24.2 us
    psum x1, blocking collectives, on_device(): lax.psum((numerator_full.reshape(local_len, width_model), denominator_ful...  21.8 us
    reduce_scatter x1, waiting for transfers between devices, on_device(): lax.psum_scatter(down_grad, 'seq', scatter_dimension=0, tiled=True)  18.4 us
  transfers between devices with their start and end apart: 9, of which 6 were waited for; matrix products, arithmetic and copies ran while one was open for 22% of the time, Pallas kernels for 0%

commit v1 on v0

--- a/solution.py
+++ b/solution.py
@@ -3,6 +3,8 @@
 import jax
 import jax.numpy as jnp
 from jax import lax
+from jax.experimental import pallas as pl
+from jax.experimental.pallas import tpu as pltpu
 from jax.sharding import PartitionSpec as P
 
 RATE_MIN = 2
@@ -349,9 +351,891 @@
     )
 
 
+MESH = pl.DeviceIdType.MESH
+LANES = 128
+LOG2E = 1.4426950408889634
+F32 = jnp.float32
+BF16 = jnp.bfloat16
+
+
+def dot_nn(left, right):
+    return lax.dot_general(left, right, (((1,), (0,)), ((), ())), preferred_element_type=F32)
+
+
+def dot_nt(left, right):
+    return lax.dot_general(left, right, (((1,), (1,)), ((), ())), preferred_element_type=F32)
+
+
+def dot_tn(left, right):
+    return lax.dot_general(left, right, (((0,), (0,)), ((), ())), preferred_element_type=F32)
+
+
+def lane_ids(width):
+    return lax.broadcasted_iota(jnp.int32, (1, width), 1)
+
+
+def slot_mask(slot, width=256):
+    ids = lane_ids(width)
+    return jnp.where((ids >= 64 * slot) & (ids < 64 * slot + 64), 1.0, 0.0).astype(F32)
+
+
+def join_halves(low_part, high_part):
+    return jnp.where(lane_ids(LANES) < 64, low_part, high_part)
+
+
+def swap_halves(tile):
+    return pltpu.roll(tile, 64, axis=1)
+
+
+def layer_kernel(
+    sizes,
+    dil_ref,
+    off_ref,
+    tok_ref,
+    cot_ref,
+    gain1_ref,
+    bias1_ref,
+    gain2_ref,
+    bias2_ref,
+    entry_hbm,
+    exit_hbm,
+    up_hbm,
+    down_hbm,
+    out_ref,
+    tgrad_ref,
+    oentry_ref,
+    oexit_ref,
+    oup_ref,
+    odown_ref,
+    ostat_ref,
+    win,
+    exit_all,
+    exit_win,
+    up_all,
+    down_all,
+    n1,
+    n2,
+    plain2,
+    inv2,
+    middle,
+    gmid,
+    gbranch,
+    mixed,
+    active,
+    ghid,
+    gn2,
+    member,
+    masks,
+    kv,
+    qb,
+    dob,
+    qmask,
+    shift,
+    invden,
+    att,
+    acc_a,
+    acc_b,
+    acc_c,
+    zmix,
+    zdq,
+    zdkv,
+    stat,
+    pc_down,
+    r1_down,
+    y_down,
+    r2_down,
+    ag_down,
+    pc_up,
+    r1_up,
+    y_up,
+    r2_up,
+    ag_up,
+    pc_entry,
+    r1_entry,
+    y_entry,
+    r2_entry,
+    ag_entry,
+    load_sem,
+    kv_ssem,
+    kv_rsem,
+    q_ssem,
+    q_rsem,
+    do_ssem,
+    do_rsem,
+    zm_ssem,
+    zm_rsem,
+    zq_ssem,
+    zq_rsem,
+    zk_ssem,
+    zk_rsem,
+    rs_s1,
+    rs_r1,
+    rs_s2,
+    rs_r2,
+    rs_zs,
+    rs_zr,
+    st_ssem,
+    st_rsem,
+):
+    T, D, HEADS, E, FF, NSEQ, NGRP = sizes
+    scale = E ** (-0.5)
+    exp_scale = scale * LOG2E
+    s = lax.axis_index("seq")
+    g = lax.axis_index("grp")
+    chip = s // 2
+    core = s % 2
+    sib = s + 1 - 2 * core
+    odd = g % 2
+    chips = NSEQ // 2
+    part = D // NGRP
+    is_odd = odd == 1
+
+    def to_seq(peer, src, dst, ssem, rsem):
+        return pltpu.make_async_remote_copy(
+            src_ref=src,
+            dst_ref=dst,
+            send_sem=ssem,
+            recv_sem=rsem,
+            device_id={"seq": peer},
+            device_id_type=MESH,
+        )
+
+    def to_grp(peer, src, dst, ssem, rsem):
+        return pltpu.make_async_remote_copy(
+            src_ref=src,
+            dst_ref=dst,
+            send_sem=ssem,
+            recv_sem=rsem,
+            device_id={"grp": peer},
+            device_id_type=MESH,
+        )
+
+    loads = []
+    for t in range(3):
+        first = pl.multiple_of(t * D + part * g - 64 * odd, LANES)
+        loads.append(
+            pltpu.make_async_copy(entry_hbm.at[:, pl.ds(first, 256)], win.at[t], load_sem.at[t])
+        )
+    loads.append(pltpu.make_async_copy(down_hbm, down_all, load_sem.at[3]))
+    loads.append(pltpu.make_async_copy(exit_hbm, exit_all, load_sem.at[4]))
+    loads.append(
+        pltpu.make_async_copy(
+            exit_hbm.at[pl.ds(pl.multiple_of(part * g, 64), part), :],
+            exit_win.at[pl.ds(64, part), :],
+            load_sem.at[5],
+        )
+    )
+    loads.append(pltpu.make_async_copy(up_hbm, up_all, load_sem.at[6]))
+    for load in loads:
+        load.start()
+    entry_all = up_all.at[:, 0 : 3 * D]
+    late_load = pltpu.make_async_copy(entry_hbm, entry_all, load_sem.at[7])
+
+    barrier = pltpu.get_barrier_semaphore()
+    for step in range(1, NSEQ):
+        pl.semaphore_signal(
+            barrier, inc=1, device_id={"seq": lax.rem(s + step, NSEQ)}, device_id_type=MESH
+        )
+    for step in range(1, NGRP):
+        pl.semaphore_signal(
+            barrier, inc=1, device_id={"grp": lax.rem(g + step, NGRP)}, device_id_type=MESH
+        )
+
+    rows = 96
+
+    def norm_one(i, carry):
+        at = pl.ds(pl.multiple_of(i * rows, rows), rows)
+        value = tok_ref[at, :].astype(F32)
+        centered = value - jnp.mean(value, axis=1, keepdims=True)
+        inverse = lax.rsqrt(jnp.mean(centered * centered, axis=1, keepdims=True) + EPS)
+        n1[at, :] = (centered * inverse * gain1_ref[...] + bias1_ref[...]).astype(BF16)
+        return carry
+
+    lax.fori_loop(0, T // rows, norm_one, 0)
+    exit_win[0:64, :] = jnp.zeros((64, D), BF16)
+
+    for t in range(3):
+        loads[t].wait()
+    lane256 = lane_ids(256)
+    q_raw = dot_nn(n1[...], win[0])
+    k_raw = dot_nn(n1[...], win[1])
+    v_raw = dot_nn(n1[...], win[2])
+    q_own = jnp.where(is_odd, pltpu.roll(q_raw, 192, axis=1), q_raw)
+    k_own = jnp.where(is_odd, pltpu.roll(k_raw, 192, axis=1), k_raw)
+    v_own = jnp.where(is_odd, v_raw, pltpu.roll(v_raw, 64, axis=1))
+    q_own = jnp.where(lane256 < 192, q_own, 0.0)
+    qb[s] = q_own.astype(BF16)
+    for h in range(3):
+        qmask[h] = (q_own * slot_mask(h)).astype(BF16)
+    kv[s, :, 0:128] = k_own[:, 0:128].astype(BF16)
+    kv[s, :, 128:256] = join_halves(k_own[:, 128:256], v_own[:, 0:128]).astype(BF16)
+    kv[s, :, 256:384] = v_own[:, 128:256].astype(BF16)
+
+    pl.semaphore_wait(barrier, NSEQ - 1 + NGRP - 1)
+
+    sends = []
+
+    def start_when(cond, copy):
+        @pl.when(cond)
+        def _():
+            copy.start()
+
+        sends.append((cond, copy))
+
+    for d in range(1, chips):
+        up_to = lax.rem(s + 2 * d, NSEQ)
+        start_when(
+            chip + d < chips,
+            to_seq(up_to, kv.at[s], kv.at[s], kv_ssem.at[d - 1], kv_rsem.at[s]),
+        )
+    start_when(core == 0, to_seq(sib, kv.at[s], kv.at[s], kv_ssem.at[3], kv_rsem.at[s]))
+    for d in range(1, chips):
+        down_to = lax.rem(s - 2 * d + NSEQ, NSEQ)
+        start_when(
+            chip - d >= 0,
+            to_seq(down_to, qb.at[s], qb.at[s], q_ssem.at[d - 1], q_rsem.at[s]),
+        )
+    start_when(core == 1, to_seq(sib, qb.at[s], qb.at[s], q_ssem.at[3], q_rsem.at[s]))
+
+    lane128 = lane_ids(LANES)
+    rate_row = jnp.ones((1, LANES), F32)
+    for i in range(NGRP):
+        rate_row = jnp.where(lane128 == i, dil_ref[i].astype(F32), rate_row)
+    local_pos = lax.broadcasted_iota(jnp.int32, (T, 1), 0).astype(F32)
+    residue = local_pos - rate_row * jnp.floor((local_pos + 0.5) / rate_row)
+    for h in range(3):
+        off_row = jnp.full((1, LANES), -1.0, F32)
+        for i in range(NGRP):
+            off_row = jnp.where(
+                lane128 == i, off_ref[i * HEADS + 3 * g + h].astype(F32), off_row
+            )
+        member[h] = jnp.where(residue == off_row, 1.0, 0.0).astype(BF16)
+    per_segment = rate_row * (T * NSEQ // RATE_MAX)
+
+    def segment_of(block):
+        return jnp.floor((jnp.full((1, LANES), block * T, jnp.int32).astype(F32) + 0.5) / per_segment)
+
+    own_segment = segment_of(s)
+
+    def build_mask(i, carry):
+        b = i // 3
+        h = i - 3 * b
+        same = jnp.where(segment_of(b) == own_segment, 1.0, 0.0)
+        count = dot_nt((member[h].astype(F32) * same).astype(BF16), member[h])
+        masks[b, h] = count.astype(BF16)
+
+        @pl.when(b == s)
+        def _():
+            row_id = lax.broadcasted_iota(jnp.int32, (T, T), 0)
+            col_id = lax.broadcasted_iota(jnp.int32, (T, T), 1)
+            masks[b, h] = jnp.where(col_id <= row_id, count + 1.0, 0.0).astype(BF16)
+            masks[NSEQ, h] = jnp.where(row_id <= col_id, count + 1.0, 0.0).astype(BF16)
+
+        return carry
+
+    lax.fori_loop(0, 3 * NSEQ, build_mask, 0)
+
+    loads[3].wait()
+
+    def cot_times_down(i, carry):
+        at = pl.ds(pl.multiple_of(i * T, T), T)
+        ghid[:, at] = dot_nt(cot_ref[...], down_all[at, :]).astype(BF16)
+        return carry
+
+    lax.fori_loop(0, FF // T, cot_times_down, 0)
+
+    acc_a[...] = jnp.zeros_like(acc_a)
+    den = shift
+    den[...] = jnp.zeros_like(den)
+
+    def forward_step(j, carry):
+        jj = j - 1 - core
+        d = jj // 2 + 1
+        which = jj % 2
+        far = jnp.where(which == 0, s - 2 * d, sib - 2 * d)
+        b = jnp.where(j == 0, s, jnp.where(jj < 0, s - 1, far))
+
+        @pl.when(j > 0)
+        def _():
+            to_seq(sib, kv.at[b], kv.at[b], kv_ssem.at[0], kv_rsem.at[b]).wait_recv()
+
+        @pl.when((jj >= 0) & (which == 0))
+        def _():
+            to_seq(sib, kv.at[b], kv.at[b], kv_ssem.at[3 + d], kv_rsem.at[b]).start()
+
+        for h in range(3):
+            score = dot_nt(qmask[h], kv[b, :, 0:256])
+            weight = jnp.exp2(score * exp_scale) * masks[b, h].astype(F32)
+            den[h] += weight[:, 0:128] + weight[:, 128:256] + weight[:, 256:384]
+            low_weight = weight.astype(BF16)
+            masks[b, h] = low_weight
+            acc_a[...] += dot_nn(low_weight, kv[b, :, 128:384]) * slot_mask(h + 1)
+        return carry
+
+    lax.fori_loop(0, s + 1, forward_step, 0)
+
+    inv_all = jnp.zeros((T, 256), F32)
+    for h in range(3):
+        inv_all = jnp.where(
+            slot_mask(h + 1) > 0.5, 1.0 / jnp.sum(den[h], axis=1, keepdims=True), inv_all
+        )
+    invden[...] = inv_all
+    att_own = acc_a[...] * inv_all
+    att[...] = att_own
+
+    def pack(target, tile_low, tile_high):
+        target[0:T, :] = tile_high.astype(BF16)
+        half = T // 2
+        target[T : T + half, :] = join_halves(
+            swap_halves(tile_low[half:T]), tile_low[0:half]
+        ).astype(BF16)
+
+    def unpack_pair(first, second, place):
+        half = T // 2
+        a_high = first[0:T, :].astype(F32)
+        a_rest = first[T : T + half, :].astype(F32)
+        b_high = second[0:T, :].astype(F32)
+        b_rest = second[T : T + half, :].astype(F32)
+        place(2, slice(0, T), b_high)
+        swapped = swap_halves(a_high)
+        place(0, slice(0, half), join_halves(swap_halves(a_rest), swapped[0:half]))
+        place(0, slice(half, T), join_halves(a_rest, swapped[half:T]))
+        place(1, slice(0, half), join_halves(swapped[0:half], b_rest))
+        place(1, slice(half, T), join_halves(swapped[half:T], swap_halves(b_rest)))
+
+    def chain_start(at, ssem, rsem):
+        start_when(g + 1 < NGRP, to_grp(lax.rem(g + 1, NGRP), at(g), at(g), ssem.at[0, 0], rsem.at[g]))
+        start_when(
+            g >= 1, to_grp(lax.rem(g + NGRP - 1, NGRP), at(g), at(g), ssem.at[0, 1], rsem.at[g])
+        )
+
+    def chain_step(d, at, ssem, rsem):
+        right = lax.rem(g + 1, NGRP)
+        left = lax.rem(g + NGRP - 1, NGRP)
+        lower = lax.rem(g - d + NGRP, NGRP)
+        upper = lax.rem(g + d, NGRP)
+
+        @pl.when(g - d >= 0)
+        def _():
+            to_grp(right, at(lower), at(lower), ssem.at[0, 0], rsem.at[lower]).wait_recv()
+
+        if d < NGRP - 1:
+            start_when(
+                (g - d >= 0) & (g + 1 < NGRP),
+                to_grp(right, at(lower), at(lower), ssem.at[d, 0], rsem.at[lower]),
+            )
+
+        @pl.when(g + d < NGRP)
+        def _():
+            to_grp(left, at(upper), at(upper), ssem.at[0, 1], rsem.at[upper]).wait_recv()
+
+        if d < NGRP - 1:
+            start_when(
+                (g + d < NGRP) & (g >= 1),
+                to_grp(left, at(upper), at(upper), ssem.at[d, 1], rsem.at[upper]),
+            )
+
+    pack(zmix.at[g], att_own[:, 0:128], att_own[:, 128:256])
+    chain_start(lambda i: zmix.at[i], zm_ssem, zm_rsem)
+
+    for d in range(1, chips):
+        slot = lax.rem(s + 2 * d, NSEQ)
+
+        @pl.when(chip + d < chips)
+        def _():
+            to_seq(sib, qb.at[slot], qb.at[slot], q_ssem.at[0], q_rsem.at[slot]).wait_recv()
+
+        start_when(
+            chip + d < chips,
+            to_seq(sib, qb.at[slot], qb.at[slot], q_ssem.at[3 + d], q_rsem.at[slot]),
+        )
+
+    for d in range(1, NGRP):
+        chain_step(d, lambda i: zmix.at[i], zm_ssem, zm_rsem)
+
+    def place_mixed(pair):
+        def place(tile, at, value):
+            first = pair * 2 * part + tile * LANES
+            mixed[at, first : first + LANES] = value.astype(BF16)
+
+        return place
+
+    for pair in range(NGRP // 2):
+        unpack_pair(zmix.at[2 * pair], zmix.at[2 * pair + 1], place_mixed(pair))
+
+    loads[4].wait()
+    middle[...] = tok_ref[...].astype(F32) + dot_nn(mixed[...], exit_all[...])
+
+    def norm_two(i, carry):
+        at = pl.ds(pl.multiple_of(i * rows, rows), rows)
+        value = middle[at, :]
+        centered = value - jnp.mean(value, axis=1, keepdims=True)
+        inverse = lax.rsqrt(jnp.mean(centered * centered, axis=1, keepdims=True) + EPS)
+        plain = centered * inverse
+        plain2[at, :] = plain
+        inv2[at, :] = jnp.broadcast_to(inverse, (rows, LANES))
+        n2[at, :] = (plain * gain2_ref[...] + bias2_ref[...]).astype(BF16)
+        return carry
+
+    lax.fori_loop(0, T // rows, norm_two, 0)
+
+    loads[6].wait()
+    gn2[...] = jnp.zeros_like(gn2)
+
+    def feed_forward(i, carry):
+        at = pl.ds(pl.multiple_of(i * T, T), T)
+        hidden = dot_nn(n2[...], up_all[:, at])
+        cdf = 0.5 + 0.5 * lax.erf(hidden * (0.5**0.5))
+        active[:, at] = (hidden * cdf).astype(BF16)
+        density = jnp.exp2(hidden * hidden * (-0.5 * LOG2E)) * 0.3989422804014327
+        low_grad = (ghid[:, at].astype(F32) * (cdf + hidden * density)).astype(BF16)
+        ghid[:, at] = low_grad
+        gn2[...] += dot_nt(low_grad, up_all[:, at])
+        return carry
+
+    lax.fori_loop(0, FF // T, feed_forward, 0)
+    late_load.start()
+
+    stat[s] = jnp.zeros((8, D), F32)
+
+    def norm_two_back(i, carry):
+        at = pl.ds(pl.multiple_of(i * rows, rows), rows)
+        upstream = gn2[at, :]
+        plain = plain2[at, :]
+        scaled = upstream * gain2_ref[...]
+        inner = (
+            scaled
+            - jnp.mean(scaled, axis=1, keepdims=True)
+            - plain * jnp.mean(scaled * plain, axis=1, keepdims=True)
+        )
+        grad = cot_ref[at, :].astype(F32) + inv2[at, 0:1] * inner
+        gmid[at, :] = grad
+        gbranch[at, :] = grad.astype(BF16)
+        stat[s, 0:1, :] += jnp.sum(upstream * plain, axis=0, keepdims=True)
+        stat[s, 1:2, :] += jnp.sum(upstream, axis=0, keepdims=True)
+        return carry
+
+    lax.fori_loop(0, T // rows, norm_two_back, 0)
+
+    loads[5].wait()
+    gmix = dot_nt(gbranch[...], exit_win[...]).astype(BF16).astype(F32)
+    numer_grad = gmix * invden[...]
+    product = numer_grad * att[...]
+    for h in range(3):
+        value = jnp.sum(product * slot_mask(h + 1), axis=1, keepdims=True)
+        shift[h] = jnp.broadcast_to(value, (T, LANES))
+        high = value.astype(BF16).astype(F32)
+        low = value - high
+        numer_grad = jnp.where(lane256 == 2 * h, high, numer_grad)
+        numer_grad = jnp.where(lane256 == 2 * h + 1, low, numer_grad)
+    dob[s] = numer_grad.astype(BF16)
+
+    for d in range(1, chips):
+        down_to = lax.rem(s - 2 * d + NSEQ, NSEQ)
+        start_when(
+            chip - d >= 0,
+            to_seq(down_to, dob.at[s], dob.at[s], do_ssem.at[d - 1], do_rsem.at[s]),
+        )
+    start_when(core == 1, to_seq(sib, dob.at[s], dob.at[s], do_ssem.at[3], do_rsem.at[s]))
+
+    width = part + 64
+    up_grad = dot_tn(n2[...], ghid[:, pl.ds(pl.multiple_of(g * D, LANES), D)])
+    for t in range(NSEQ):
+        pc_up[t % 2, t // 2] = up_grad[96 * t : 96 * t + 96, :].astype(BF16)
+
+    @pl.when(g < 3)
+    def _():
+        cols = pl.ds(pl.multiple_of(lax.rem(g, 3) * width, LANES), width)
+
+        def down_piece(t, carry):
+            at = pl.ds(pl.multiple_of(t * T, T), T)
+            pc_down[t % 2, t // 2] = dot_tn(active[:, at], cot_ref[:, cols]).astype(BF16)
+            return carry
+
+        lax.fori_loop(0, NSEQ, down_piece, 0)
+
+    @pl.when(g == 3)
+    def _():
+        exit_grad = dot_tn(mixed[...], gbranch[...]).astype(BF16)
+        for t in range(NSEQ):
+            for i in range(3):
+                pc_down[t % 2, t // 2, 96 * i : 96 * i + 96, :] = exit_grad[
+                    96 * t : 96 * t + 96, width * i : width * i + width
+                ]
+            pc_down[t % 2, t // 2, 288:384, :] = jnp.zeros((96, width), BF16)
+
+    def reduce_start(i, pieces, first_in):
+        start_when(
+            core >= 0,
+            to_seq(sib, pieces.at[1 - core], first_in, rs_s1.at[i], rs_r1.at[i]),
+        )
+
+    def reduce_pass(i, pieces, first_in, total, second_in):
+        to_seq(sib, pieces.at[core], first_in, rs_s1.at[i], rs_r1.at[i]).wait_recv()
+        for cc in range(chips):
+            total[cc] = (pieces[core, cc].astype(F32) + first_in[cc].astype(F32)).astype(BF16)
+        for d in range(1, chips):
+            to_chip = lax.rem(chip + d, chips)
+            start_when(
+                core >= 0,
+                to_seq(
+                    2 * to_chip + core,
+                    total.at[to_chip],
+                    second_in.at[chip],
+                    rs_s2.at[i, d - 1],
+                    rs_r2.at[i, chip],
+                ),
+            )
+
+    def reduce_end(i, total, second_in, gathered):
+        result = total[chip].astype(F32)
+        for d in range(1, chips):
+            slot = lax.rem(chip + d, chips)
+            to_seq(
+                sib, second_in.at[slot], second_in.at[slot], rs_s1.at[i], rs_r2.at[i, slot]
+            ).wait_recv()
+            result = result + second_in[slot].astype(F32)
+        gathered[g] = result.astype(BF16)
+        chain_start(lambda j: gathered.at[j], rs_zs.at[i], rs_zr.at[i])
+
+    reduce_start(0, pc_up, r1_up)
+    reduce_start(1, pc_down, r1_down)
+
+    for h in range(3):
+        qmask[h] = (dob[s].astype(F32) * slot_mask(h + 1)).astype(BF16)
+    acc_a[...] = jnp.zeros_like(acc_a)
+
+    def query_side(b, carry):
+        for h in range(3):
+            pressure = dot_nt(qmask[h], kv[b, :, 128:384])
+            row_shift = shift[h]
+            row_shift = jnp.concatenate([row_shift, row_shift, row_shift], axis=1)
+            slope = (masks[b, h].astype(F32) * (pressure - row_shift)).astype(BF16)
+            acc_a[...] += dot_nn(slope, kv[b, :, 0:256]) * slot_mask(h)
+        return carry
+
+    lax.fori_loop(0, s + 1, query_side, 0)
+    dq = pltpu.roll(acc_a[...] * scale, 64, axis=1)
+    pack(zdq.at[g], dq[:, 0:128], dq[:, 128:256])
+    chain_start(lambda i: zdq.at[i], zq_ssem, zq_rsem)
+
+    reduce_pass(0, pc_up, r1_up, y_up, r2_up)
+    reduce_pass(1, pc_down, r1_down, y_down, r2_down)
+
+    acc_b[...] = jnp.zeros_like(acc_b)
+    acc_c[...] = jnp.zeros_like(acc_c)
+    v_tile = kv[s, :, 128:384].astype(F32)
+    k_tile = kv[s, :, 0:256].astype(F32)
+    for h in range(3):
+        qmask[h] = (k_tile * slot_mask(h)).astype(BF16)
+        minus = jnp.where((lane256 == 2 * h) | (lane256 == 2 * h + 1), -1.0, 0.0)
+        qmask[3 + h] = (v_tile * slot_mask(h + 1) + minus).astype(BF16)
+
+    def key_side(j, carry):
+        jj = j - 2 + core
+        d = jj // 2 + 1
+        which = jj % 2
+        far = jnp.where(which == 0, s + 2 * d, sib + 2 * d)
+        b = jnp.where(j == 0, s, jnp.where(jj < 0, s + 1, far))
+
+        @pl.when(j > 0)
+        def _():
+            to_seq(sib, dob.at[b], dob.at[b], do_ssem.at[0], do_rsem.at[b]).wait_recv()
+
+        @pl.when((jj >= 0) & (which == 0))
+        def _():
+            to_seq(sib, dob.at[b], dob.at[b], do_ssem.at[3 + d], do_rsem.at[b]).start()
+
+        @pl.when((j > 0) & ((jj < 0) | (which == 1)))
+        def _():
+            to_seq(sib, qb.at[b], qb.at[b], q_ssem.at[0], q_rsem.at[b]).wait_recv()
+
+        at = jnp.where(j == 0, NSEQ, b)
+        for h in range(3):
+            score = dot_nt(qmask[h], qb[b])
+            weight = jnp.exp2(score * exp_scale) * masks[at, h].astype(F32)
+            pressure = dot_nt(qmask[3 + h], dob[b])
+            slope = (weight * pressure).astype(BF16)
+            acc_b[...] += dot_nn(slope, qb[b]) * slot_mask(h)
+            acc_c[...] += dot_nn(weight.astype(BF16), dob[b]) * slot_mask(h + 1)
+        return carry
+
+    lax.fori_loop(0, NSEQ - s, key_side, 0)
+
+    dk = pltpu.roll(acc_b[...] * scale, 64, axis=1)
+    pack(zdkv.at[g, 0], dk[:, 0:128], dk[:, 128:256])
+    dv = acc_c[...]
+    pack(zdkv.at[g, 1], dv[:, 0:128], dv[:, 128:256])
+    chain_start(lambda i: zdkv.at[i], zk_ssem, zk_rsem)
+
+    dfull = ghid.at[:, 0 : 3 * D]
+    dpack = ghid.at[:, 3 * D : 3 * D + 640]
+    dpack[:, 0:128] = join_halves(swap_halves(dq[:, 0:128]), swap_halves(dq[:, 128:256])).astype(BF16)
+    dpack[:, 128:256] = join_halves(swap_halves(dq[:, 128:256]), dk[:, 0:128]).astype(BF16)
+    dpack[:, 256:384] = dk[:, 128:256].astype(BF16)
+    dpack[:, 384:512] = join_halves(swap_halves(dv[:, 0:128]), swap_halves(dv[:, 128:256])).astype(BF16)
+    dpack[:, 512:640] = join_halves(swap_halves(dv[:, 128:256]), jnp.zeros((T, LANES), F32)).astype(BF16)
+    entry_grad = dot_tn(n1[...], dpack[...])
+    for t in range(NSEQ):
+        pc_entry[t % 2, t // 2] = entry_grad[96 * t : 96 * t + 96, :].astype(BF16)
+    reduce_start(2, pc_entry, r1_entry)
+
+    reduce_end(0, y_up, r2_up, ag_up)
+    reduce_end(1, y_down, r2_down, ag_down)
+    for d in range(1, NGRP):
+        chain_step(d, lambda i: zdq.at[i], zq_ssem, zq_rsem)
+    reduce_pass(2, pc_entry, r1_entry, y_entry, r2_entry)
+    for d in range(1, NGRP):
+        chain_step(d, lambda i: zdkv.at[i], zk_ssem, zk_rsem)
+
+    def place_grad(first_col):
+        def place(tile, at, value):
+            first = first_col + tile * LANES
+            dfull[at, first : first + LANES] = value.astype(BF16)
+
+        return place
+
+    for pair in range(NGRP // 2):
+        first_col = pair * 2 * part
+        unpack_pair(zdq.at[2 * pair], zdq.at[2 * pair + 1], place_grad(first_col))
+        for t in range(2):
+            unpack_pair(
+                zdkv.at[2 * pair, t], zdkv.at[2 * pair + 1, t], place_grad((t + 1) * D + first_col)
+            )
+
+    out_ref[...] = (middle[...] + dot_nn(active[...], down_all[...])).astype(BF16)
+    reduce_end(2, y_entry, r2_entry, ag_entry)
+    late_load.wait()
+    gn2[...] = dot_nt(dfull[...], up_all[:, 0 : 3 * D])
+
+    def norm_one_back(i, carry):
+        at = pl.ds(pl.multiple_of(i * rows, rows), rows)
+        value = tok_ref[at, :].astype(F32)
+        centered = value - jnp.mean(value, axis=1, keepdims=True)
+        inverse = lax.rsqrt(jnp.mean(centered * centered, axis=1, keepdims=True) + EPS)
+        plain = centered * inverse
+        upstream = gn2[at, :]
+        scaled = upstream * gain1_ref[...]
+        inner = (
+            scaled
+            - jnp.mean(scaled, axis=1, keepdims=True)
+            - plain * jnp.mean(scaled * plain, axis=1, keepdims=True)
+        )
+        tgrad_ref[at, :] = (gmid[at, :] + inverse * inner).astype(BF16)
+        stat[s, 2:3, :] += jnp.sum(upstream * plain, axis=0, keepdims=True)
+        stat[s, 3:4, :] += jnp.sum(upstream, axis=0, keepdims=True)
+        return carry
+
+    lax.fori_loop(0, T // rows, norm_one_back, 0)
+    for step in range(1, NSEQ):
+        peer = lax.rem(s + step, NSEQ)
+        start_when(
+            core >= 0, to_seq(peer, stat.at[s], stat.at[s], st_ssem.at[step - 1], st_rsem.at[s])
+        )
+
+    for d in range(1, NGRP):
+        chain_step(d, lambda i: ag_up.at[i], rs_zs.at[0], rs_zr.at[0])
+    for i in range(NGRP):
+        oup_ref[:, D * i : D * i + D] = ag_up[i]
+    for d in range(1, NGRP):
+        chain_step(d, lambda i: ag_down.at[i], rs_zs.at[1], rs_zr.at[1])
+    for i in range(3):
+        odown_ref[:, width * i : width * i + width] = ag_down[i]
+        oexit_ref[:, width * i : width * i + width] = ag_down[3, 96 * i : 96 * i + 96, :]
+    for d in range(1, NGRP):
+        chain_step(d, lambda i: ag_entry.at[i], rs_zs.at[2], rs_zr.at[2])
+    for pair in range(NGRP // 2):
+        a = ag_entry[2 * pair].astype(F32)
+        b = ag_entry[2 * pair + 1].astype(F32)
+        first = pair * 2 * part
+        tiles = (
+            (0, a[:, 0:128]),
+            (1, join_halves(a[:, 128:256], swap_halves(b[:, 0:128]))),
+            (2, join_halves(swap_halves(b[:, 0:128]), swap_halves(b[:, 128:256]))),
+            (6, join_halves(swap_halves(a[:, 128:256]), swap_halves(a[:, 256:384]))),
+            (7, join_halves(swap_halves(a[:, 256:384]), b[:, 128:256])),
+            (8, b[:, 256:384]),
+            (12, a[:, 384:512]),
+            (13, join_halves(a[:, 512:640], swap_halves(b[:, 384:512]))),
+            (14, join_halves(swap_halves(b[:, 384:512]), swap_halves(b[:, 512:640]))),
+        )
+        for tile, value in tiles:
+            at = tile * LANES + first
+            oentry_ref[:, at : at + LANES] = value.astype(BF16)
+
+    for step in range(1, NSEQ):
+        slot = lax.rem(s + step, NSEQ)
+        to_seq(sib, stat.at[slot], stat.at[slot], st_ssem.at[0], st_rsem.at[slot]).wait_recv()
+    total_stat = stat[0]
+    for i in range(1, NSEQ):
+        total_stat = total_stat + stat[i]
+    ostat_ref[...] = total_stat
+
+    for cond, copy in sends:
+
+        @pl.when(cond)
+        def _(copy=copy):
+            copy.wait_send()
+
+    for d in range(1, chips):
+
+        @pl.when(chip - d >= 0)
+        def _(d=d):
+            slot = lax.rem(s - 2 * d + NSEQ, NSEQ)
+            to_seq(sib, kv.at[slot], kv.at[slot], kv_ssem.at[3 + d], kv_rsem.at[slot]).wait_send()
+
+        @pl.when(chip + d < chips)
+        def _(d=d):
+            slot = lax.rem(s + 2 * d, NSEQ)
+            to_seq(sib, dob.at[slot], dob.at[slot], do_ssem.at[3 + d], do_rsem.at[slot]).wait_send()
+
+
+def fast_on_device(
+    seq_count,
+    tokens,
+    cotangent,
+    entry_weight,
+    exit_weight,
+    up_weight,
+    down_weight,
+    first_gain,
+    first_bias,
+    second_gain,
+    second_bias,
+    dilations,
+    offsets,
+):
+    T, D = tokens.shape
+    NGRP, HEADS = offsets.shape
+    FF = up_weight.shape[1]
+    E = D // HEADS
+    NSEQ = seq_count
+    chips = NSEQ // 2
+    sizes = (T, D, HEADS, E, FF, NSEQ, NGRP)
+    share = T * 3 // 2
+    vmem = pl.BlockSpec(memory_space=pltpu.VMEM)
+    smem = pl.BlockSpec(memory_space=pltpu.SMEM)
+    anywhere = pl.BlockSpec(memory_space=pl.ANY)
+    dma = pltpu.SemaphoreType.DMA
+    scratch = [
+        pltpu.VMEM((3, D, 256), BF16),
+        pltpu.VMEM((D, D), BF16),
+        pltpu.VMEM((256, D), BF16),
+        pltpu.VMEM((D, FF), BF16),
+        pltpu.VMEM((FF, D), BF16),
+        pltpu.VMEM((T, D), BF16),
+        pltpu.VMEM((T, D), BF16),
+        pltpu.VMEM((T, D), F32),
+        pltpu.VMEM((T, LANES), F32),
+        pltpu.VMEM((T, D), F32),
+        pltpu.VMEM((T, D), F32),
+        pltpu.VMEM((T, D), BF16),
+        pltpu.VMEM((T, D), BF16),
+        pltpu.VMEM((T, FF), BF16),
+        pltpu.VMEM((T, FF), BF16),
+        pltpu.VMEM((T, D), F32),
+        pltpu.VMEM((3, T, LANES), BF16),
+        pltpu.VMEM((NSEQ + 1, 3, T, T), BF16),
+        pltpu.VMEM((NSEQ, T, 384), BF16),
+        pltpu.VMEM((NSEQ, T, 256), BF16),
+        pltpu.VMEM((NSEQ, T, 256), BF16),
+        pltpu.VMEM((6, T, 256), BF16),
+        pltpu.VMEM((3, T, LANES), F32),
+        pltpu.VMEM((T, 256), F32),
+        pltpu.VMEM((T, 256), F32),
+        pltpu.VMEM((T, 256), F32),
+        pltpu.VMEM((T, 256), F32),
+        pltpu.VMEM((T, 256), F32),
+        pltpu.VMEM((NGRP, share, LANES), BF16),
+        pltpu.VMEM((NGRP, share, LANES), BF16),
+        pltpu.VMEM((NGRP, 2, share, LANES), BF16),
+        pltpu.VMEM((NSEQ, 8, D), F32),
+    ]
+    for rows, cols in ((T, 256), (96, D), (96, 640)):
+        scratch += [
+            pltpu.VMEM((2, chips, rows, cols), BF16),
+            pltpu.VMEM((chips, rows, cols), BF16),
+            pltpu.VMEM((chips, rows, cols), BF16),
+            pltpu.VMEM((chips, rows, cols), BF16),
+            pltpu.VMEM((NGRP, rows, cols), BF16),
+        ]
+    scratch += [
+        dma((8,)),
+        dma((7,)),
+        dma((NSEQ,)),
+        dma((7,)),
+        dma((NSEQ,)),
+        dma((7,)),
+        dma((NSEQ,)),
+        dma((3, 2)),
+        dma((NGRP,)),
+        dma((3, 2)),
+        dma((NGRP,)),
+        dma((3, 2)),
+        dma((NGRP,)),
+        dma((3,)),
+        dma((3,)),
+        dma((3, 3)),
+        dma((3, chips)),
+        dma((3, 3, 2)),
+        dma((3, NGRP)),
+        dma((NSEQ - 1,)),
+        dma((NSEQ,)),
+    ]
+    out_shape = (
+        jax.ShapeDtypeStruct((T, D), BF16),
+        jax.ShapeDtypeStruct((T, D), BF16),
+        jax.ShapeDtypeStruct((96, 3 * D), BF16),
+        jax.ShapeDtypeStruct((96, D), BF16),
+        jax.ShapeDtypeStruct((96, FF), BF16),
+        jax.ShapeDtypeStruct((T, D), BF16),
+        jax.ShapeDtypeStruct((8, D), F32),
+    )
+    output, token_grad, entry_grad, exit_grad, up_grad, down_grad, stats = pl.pallas_call(
+        partial(layer_kernel, sizes),
+        out_shape=out_shape,
+        in_specs=[smem] * 2 + [vmem] * 6 + [anywhere] * 4,
+        out_specs=tuple([vmem] * 7),
+        scratch_shapes=scratch,
+        compiler_params=pltpu.CompilerParams(
+            collective_id=0, has_side_effects=True, vmem_limit_bytes=63 * 1024 * 1024
+        ),
+        name="layer",
+    )(
+        dilations,
+        offsets.reshape(-1),
+        tokens,
+        cotangent,
+        first_gain.reshape(1, D),
+        first_bias.reshape(1, D),
+        second_gain.reshape(1, D),
+        second_bias.reshape(1, D),
+        entry_weight,
+        exit_weight,
+        up_weight,
+        down_weight,
+    )
+    start = lax.axis_index("seq") * (D // NSEQ)
+    own = lax.dynamic_slice_in_dim(stats, start, D // NSEQ, 1)
+    return (
+        output,
+        token_grad,
+        entry_grad.astype(F32),
+        exit_grad.astype(F32),
+        up_grad.astype(F32),
+        down_grad.astype(F32),
+        own[2],
+        own[3],
+        own[0],
+        own[1],
+    )
+
+
 def solution(mesh):
+    seq_count = mesh.shape["seq"]
+    fast = seq_count == 8 and mesh.shape["grp"] == 4
     return jax.shard_map(
-        on_device,
+        partial(fast_on_device, seq_count) if fast else on_device,
         mesh=mesh,
         in_specs=(P("seq", None), P("seq", None), P(), P(), P(), P(), P(), P(), P(), P(), P(), P()),
         out_specs=(

time: 626 us -> 141 us (0.23); the launches traced: 618 us -> 141 us
  waiting for transfers between devices: 196 us -> 0 us
  blocking collectives: 172 us -> 0 us
  matrix products: 151 us -> 0 us
  Pallas kernels: 0 us -> 125 us
  local copies, waits for them, and re-layouts: 51.3 us -> 9.41 us
  other arithmetic: 28 us -> 6.03 us
  between operations: 17.8 us -> 0.7 us
    dot_general x35 -> x0, matrix products: 151 us -> none  [the longest x1 14.1 us: on_device(): jnp.dot(cotangent, down_weight.T, preferred_element_type=jnp.float32)]
    psum x2 -> x0, blocking collectives: 148 us -> none  [the longest x1 126 us: on_device(): summed = lax.psum(grad_packed, 'grp').astype(jnp.bfloat16)]
    pallas_call x0 -> x1, Pallas kernels: none -> 125 us  [fast_on_device(): pl.pallas_call(partial(layer_kernel, sizes), out_shape=out_shape, in_spec...]
    reduce_scatter x4 -> x0, waiting for transfers between devices: 88.4 us -> none  [the longest x1 70 us: on_device(): lax.psum_scatter(entry_grad, 'seq', scatter_dimension=0, tiled=True)]
    unnamed x11 -> x0, waiting for transfers between devices: 50.2 us -> none
    psum x1 -> x0, waiting for transfers between devices: 31.8 us -> none  [on_device(): lax.psum((numerator_full.reshape(local_len, width_model), denominator_ful...]
    all_gather x2 -> x0, waiting for transfers between devices: 25.7 us -> none  [the longest x1 16 us: on_device(): lax.all_gather(value_sp, 'seq', axis=0, tiled=True)]
    unnamed x89 -> x10, local copies, waits for them, and re-layouts: 27.3 us -> 1.65 us
  transfers between devices with their start and end apart: 9 -> 0, of which waited for: 6 -> 0; matrix products, arithmetic and copies ran while one was open for 22% -> 0% of each run, Pallas kernels for 0% -> 0%
where the time goes in v1:
time: 141 us
  Pallas kernels  125 us (89%)
  local copies, waits for them, and re-layouts  9.41 us (7%)
  other arithmetic  6.03 us (4%)
    pallas_call x1, Pallas kernels, fast_on_device(): pl.pallas_call(partial(layer_kernel, sizes), out_shape=out_shape, in_spec...  125 us

profile of v1, /device:TPU:0, one launch (start us, length us, event | category | flops | bytes accessed | tf_op | source)
XLA Modules:
  0.0 140.7 jit_solution(8572411269666007201)
XLA Ops:
  0.6 1.3 reshape.36.gain1_ref
  1.9 1.3 reshape.37.bias1_ref
  3.2 1.3 reshape.38.gain2_ref
  4.4 1.3 reshape.39.bias2_ref
  5.7 1.3 reshape.35.off_ref
  7.0 124.5 %layer.1 = (bf16[384,768]{1,0:T(8,128)(2,1)}, bf16[384,768]{1,0:T(8,128)(2,1)}, bf16[96,2304]{1,0:T(8,128)(2,1)}, bf16[96,768]{1,0:T(8,128)(2,1)}, bf16[96,3072]...) custom-call(s32[4]{0:T(128)} %dil_ref.1, s32[48]{0:T(128)} %reshape.35.off_ref, bf16[384,768]{1,0:T(8,128)(2,1)} %tok_ref.1, ...), custom_call_target="tpu_custom_call" | custom-call | tf_op jit(solution)/shard_map/layer/pallas_call | solution.py:1194
  131.5 0.0 copy-start.2
  131.5 0.0 copy-start.3
  131.5 0.0 copy-start.1
  131.5 0.0 copy-start
  131.6 0.9 constant_dynamic-slice_fusion
  132.5 0.5 slice_bitcast_fusion
  133.0 2.2 %convert_element_type.14 = f32[96,3072]{1,0:T(8,128)} convert(bf16[96,3072]{1,0:T(8,128)(2,1)} %get-tuple-element.21) | non-fusion elementwise | flops 294912 | bytes 1769472 | tf_op jit(solution)/shard_map/convert_element_type | solution.py:1225
  135.2 2.2 %convert_element_type.15 = f32[384,768]{1,0:T(8,128)} convert(bf16[384,768]{1,0:T(8,128)(2,1)} %get-tuple-element.22) | non-fusion elementwise | flops 294912 | bytes 1769472 | tf_op jit(solution)/shard_map/convert_element_type | solution.py:1226
  137.3 0.0 copy-done.2
  137.3 1.0 convert_element_type.12
  138.3 0.0 copy-done.3
  138.3 0.7 convert_element_type.13
  139.0 0.0 copy-done.1
  139.0 0.8 copy.24
  139.8 0.0 copy-done
  139.8 0.8 copy.25
Async XLA Ops:
  131.5 5.8 %copy-start.2 = (bf16[96,2304]{1,0:T(8,128)(2,1)S(1)}, bf16[96,2304]{1,0:T(8,128)(2,1)}, u32[]{:S(2)}) copy-start(bf16[96,2304]{1,0:T(8,128)(2,1)} %get-tuple-element.19) | copy-start | bytes 1327108
  131.5 6.8 %copy-start.3 = (bf16[96,768]{1,0:T(8,128)(2,1)S(1)}, bf16[96,768]{1,0:T(8,128)(2,1)}, u32[]{:S(2)}) copy-start(bf16[96,768]{1,0:T(8,128)(2,1)} %get-tuple-element.20) | copy-start | bytes 442372
  131.5 7.5 %copy-start.1 = (bf16[384,768]{1,0:T(8,128)(2,1)S(1)}, bf16[384,768]{1,0:T(8,128)(2,1)}, u32[]{:S(2)}) copy-start(bf16[384,768]{1,0:T(8,128)(2,1)} %get-tuple-element.38) | copy-start | bytes 1769476
  131.5 8.3 %copy-start = (bf16[384,768]{1,0:T(8,128)(2,1)S(1)}, bf16[384,768]{1,0:T(8,128)(2,1)}, u32[]{:S(2)}) copy-start(bf16[384,768]{1,0:T(8,128)(2,1)} %get-tuple-element.39) | copy-start | bytes 1769476

commit v2 on v1

--- a/solution.py
+++ b/solution.py
@@ -489,6 +489,10 @@
     chips = NSEQ // 2
     part = D // NGRP
     is_odd = odd == 1
+    gain1 = gain1_ref[...].reshape(1, D)
+    bias1 = bias1_ref[...].reshape(1, D)
+    gain2 = gain2_ref[...].reshape(1, D)
+    bias2 = bias2_ref[...].reshape(1, D)
 
     def to_seq(peer, src, dst, ssem, rsem):
         return pltpu.make_async_remote_copy(
@@ -548,7 +552,7 @@
         value = tok_ref[at, :].astype(F32)
         centered = value - jnp.mean(value, axis=1, keepdims=True)
         inverse = lax.rsqrt(jnp.mean(centered * centered, axis=1, keepdims=True) + EPS)
-        n1[at, :] = (centered * inverse * gain1_ref[...] + bias1_ref[...]).astype(BF16)
+        n1[at, :] = (centered * inverse * gain1 + bias1).astype(BF16)
         return carry
 
     lax.fori_loop(0, T // rows, norm_one, 0)
@@ -607,7 +611,7 @@
         off_row = jnp.full((1, LANES), -1.0, F32)
         for i in range(NGRP):
             off_row = jnp.where(
-                lane128 == i, off_ref[i * HEADS + 3 * g + h].astype(F32), off_row
+                lane128 == i, off_ref[i, 3 * g + h].astype(F32), off_row
             )
         member[h] = jnp.where(residue == off_row, 1.0, 0.0).astype(BF16)
     per_segment = rate_row * (T * NSEQ // RATE_MAX)
@@ -774,7 +778,7 @@
         plain = centered * inverse
         plain2[at, :] = plain
         inv2[at, :] = jnp.broadcast_to(inverse, (rows, LANES))
-        n2[at, :] = (plain * gain2_ref[...] + bias2_ref[...]).astype(BF16)
+        n2[at, :] = (plain * gain2 + bias2).astype(BF16)
         return carry
 
     lax.fori_loop(0, T // rows, norm_two, 0)
@@ -802,7 +806,7 @@
         at = pl.ds(pl.multiple_of(i * rows, rows), rows)
         upstream = gn2[at, :]
         plain = plain2[at, :]
-        scaled = upstream * gain2_ref[...]
+        scaled = upstream * gain2
         inner = (
             scaled
             - jnp.mean(scaled, axis=1, keepdims=True)
@@ -1015,7 +1019,7 @@
         inverse = lax.rsqrt(jnp.mean(centered * centered, axis=1, keepdims=True) + EPS)
         plain = centered * inverse
         upstream = gn2[at, :]
-        scaled = upstream * gain1_ref[...]
+        scaled = upstream * gain1
         inner = (
             scaled
             - jnp.mean(scaled, axis=1, keepdims=True)
@@ -1088,6 +1092,73 @@
         def _(d=d):
             slot = lax.rem(s + 2 * d, NSEQ)
             to_seq(sib, dob.at[slot], dob.at[slot], do_ssem.at[3 + d], do_rsem.at[slot]).wait_send()
+
+
+def finish_kernel(
+    out_in,
+    tgrad_in,
+    entry_in,
+    exit_in,
+    up_in,
+    down_in,
+    stat_in,
+    out_hbm,
+    tgrad_hbm,
+    entry_hbm,
+    exit_hbm,
+    up_hbm,
+    down_hbm,
+    fgain_ref,
+    fbias_ref,
+    sgain_ref,
+    sbias_ref,
+    out_low,
+    tgrad_low,
+    down_low,
+    up_low,
+    entry_low,
+    exit_low,
+    stat_low,
+    down_full,
+    up_full,
+    entry_full,
+    exit_full,
+    sems,
+):
+    plans = (
+        (down_in, down_low, down_full, down_hbm),
+        (up_in, up_low, up_full, up_hbm),
+        (entry_in, entry_low, entry_full, entry_hbm),
+        (exit_in, exit_low, exit_full, exit_hbm),
+        (out_in, out_low, out_low, out_hbm),
+        (tgrad_in, tgrad_low, tgrad_low, tgrad_hbm),
+    )
+    loads = [
+        pltpu.make_async_copy(source, low, sems.at[6 + i])
+        for i, (source, low, _, _) in enumerate(plans)
+    ]
+    stat_load = pltpu.make_async_copy(stat_in, stat_low, sems.at[12])
+    for copy in [*loads, stat_load]:
+        copy.start()
+    copies = []
+    for i, (_, low, full, target) in enumerate(plans):
+        loads[i].wait()
+        if full is not low:
+            full[...] = low[...].astype(F32)
+        copy = pltpu.make_async_copy(full, target, sems.at[i])
+        copy.start()
+        copies.append(copy)
+    stat_load.wait()
+    width = stat_low.shape[1]
+    part = fgain_ref.shape[0]
+    first = lax.axis_index("seq") * part
+    turned = pltpu.roll(stat_low[...], lax.rem(width - first, width), axis=1)
+    fgain_ref[...] = turned[2:3, 0:part].reshape(part)
+    fbias_ref[...] = turned[3:4, 0:part].reshape(part)
+    sgain_ref[...] = turned[0:1, 0:part].reshape(part)
+    sbias_ref[...] = turned[1:2, 0:part].reshape(part)
+    for copy in copies:
+        copy.wait()
 
 
 def fast_on_device(
@@ -1203,32 +1274,49 @@
         name="layer",
     )(
         dilations,
-        offsets.reshape(-1),
+        offsets,
         tokens,
         cotangent,
-        first_gain.reshape(1, D),
-        first_bias.reshape(1, D),
-        second_gain.reshape(1, D),
-        second_bias.reshape(1, D),
+        first_gain,
+        first_bias,
+        second_gain,
+        second_bias,
         entry_weight,
         exit_weight,
         up_weight,
         down_weight,
     )
-    start = lax.axis_index("seq") * (D // NSEQ)
-    own = lax.dynamic_slice_in_dim(stats, start, D // NSEQ, 1)
-    return (
-        output,
-        token_grad,
-        entry_grad.astype(F32),
-        exit_grad.astype(F32),
-        up_grad.astype(F32),
-        down_grad.astype(F32),
-        own[2],
-        own[3],
-        own[0],
-        own[1],
-    )
+    part = D // NSEQ
+    finish_shape = (
+        jax.ShapeDtypeStruct((T, D), BF16),
+        jax.ShapeDtypeStruct((T, D), BF16),
+        jax.ShapeDtypeStruct((part, 3 * D), F32),
+        jax.ShapeDtypeStruct((part, D), F32),
+        jax.ShapeDtypeStruct((part, FF), F32),
+        jax.ShapeDtypeStruct((T, D), F32),
+    ) + tuple([jax.ShapeDtypeStruct((part,), F32)] * 4)
+    return pl.pallas_call(
+        finish_kernel,
+        out_shape=finish_shape,
+        in_specs=[anywhere] * 7,
+        out_specs=tuple([anywhere] * 6 + [vmem] * 4),
+        scratch_shapes=[
+            pltpu.VMEM((T, D), BF16),
+            pltpu.VMEM((T, D), BF16),
+            pltpu.VMEM((T, D), BF16),
+            pltpu.VMEM((part, FF), BF16),
+            pltpu.VMEM((part, 3 * D), BF16),
+            pltpu.VMEM((part, D), BF16),
+            pltpu.VMEM((8, D), F32),
+            pltpu.VMEM((T, D), F32),
+            pltpu.VMEM((part, FF), F32),
+            pltpu.VMEM((part, 3 * D), F32),
+            pltpu.VMEM((part, D), F32),
+            dma((13,)),
+        ],
+        compiler_params=pltpu.CompilerParams(vmem_limit_bytes=62 * 1024 * 1024),
+        name="finish",
+    )(output, token_grad, entry_grad, exit_grad, up_grad, down_grad, stats)
 
 
 def solution(mesh):

time: 141 us -> 130 us (0.922)
  local copies, waits for them, and re-layouts: 9.41 us -> 0 us
  other arithmetic: 6.03 us -> 0 us
  Pallas kernels: 125 us -> 129 us
    reshape x5 -> x0, local copies, waits for them, and re-layouts: 6.34 us -> none  [the longest x1 1.27 us: fast_on_device(): offsets.reshape(-1)]
    convert_element_type x4 -> x0, other arithmetic: 6.03 us -> none  [the longest x1 2.18 us: fast_on_device(): up_grad.astype(F32)]
    pallas_call x0 -> x1, Pallas kernels: none -> 3.95 us  [fast_on_device(): pl.pallas_call(finish_kernel, out_shape=finish_shape, in_specs=[anywhere]...]
    unnamed x10 -> x0, local copies, waits for them, and re-layouts: 1.65 us -> none
where the time goes in v2:
time: 130 us
  Pallas kernels  129 us (99%)
    pallas_call x1, Pallas kernels, fast_on_device(): pl.pallas_call(partial(layer_kernel, sizes), out_shape=out_shape, in_spec...  125 us
    pallas_call x1, Pallas kernels, fast_on_device(): pl.pallas_call(finish_kernel, out_shape=finish_shape, in_specs=[anywhere]...  3.95 us

profile of v2, /device:TPU:0, one launch (start us, length us, event | category | flops | bytes accessed | tf_op | source)
XLA Modules:
  0.0 129.5 jit_solution(15461432231601125816)
XLA Ops:
  0.6 124.8 %layer.1 = (bf16[384,768]{1,0:T(8,128)(2,1)}, bf16[384,768]{1,0:T(8,128)(2,1)}, bf16[96,2304]{1,0:T(8,128)(2,1)}, bf16[96,768]{1,0:T(8,128)(2,1)}, bf16[96,3072]...) custom-call(s32[4]{0:T(128)} %dil_ref.1, s32[4,12]{1,0:T(4,128)} %off_ref.1, bf16[384,768]{1,0:T(8,128)(2,1)} %tok_ref.1, ...), custom_call_target="tpu_custom_call" | custom-call | tf_op jit(solution)/shard_map/layer/pallas_call | solution.py:1265
  125.4 4.0 %finish.1 = (bf16[384,768]{1,0:T(8,128)(2,1)}, bf16[384,768]{1,0:T(8,128)(2,1)}, f32[96,2304]{1,0:T(8,128)}, f32[96,768]{1,0:T(8,128)}, f32[96,3072]{1,0:T(8,128...) custom-call(bf16[384,768]{1,0:T(8,128)(2,1)} %get-tuple-element.17.out_in, ...), custom_call_target="tpu_custom_call" | custom-call | tf_op jit(solution)/shard_map/finish/pallas_call | solution.py:1298

commit v3 on v2

--- a/solution.py
+++ b/solution.py
@@ -415,8 +415,6 @@
     down_all,
     n1,
     n2,
-    plain2,
-    inv2,
     middle,
     gmid,
     gbranch,
@@ -437,24 +435,26 @@
     acc_b,
     acc_c,
     zmix,
-    zdq,
-    zdkv,
+    drecv,
+    tz,
     stat,
+    stat_z,
+    pc_up,
+    r1_up,
+    r2_up,
+    ag_up,
     pc_down,
     r1_down,
-    y_down,
     r2_down,
     ag_down,
-    pc_up,
-    r1_up,
-    y_up,
-    r2_up,
-    ag_up,
-    pc_entry,
-    r1_entry,
-    y_entry,
-    r2_entry,
-    ag_entry,
+    pc_eq,
+    r1_eq,
+    r2_eq,
+    ag_eq,
+    pc_ekv,
+    r1_ekv,
+    r2_ekv,
+    ag_ekv,
     load_sem,
     kv_ssem,
     kv_rsem,
@@ -464,10 +464,10 @@
     do_rsem,
     zm_ssem,
     zm_rsem,
-    zq_ssem,
-    zq_rsem,
-    zk_ssem,
-    zk_rsem,
+    zd_ssem,
+    zd_rsem,
+    zt_ssem,
+    zt_rsem,
     rs_s1,
     rs_r1,
     rs_s2,
@@ -476,6 +476,8 @@
     rs_zr,
     st_ssem,
     st_rsem,
+    sz_ssem,
+    sz_rsem,
 ):
     T, D, HEADS, E, FF, NSEQ, NGRP = sizes
     scale = E ** (-0.5)
@@ -532,8 +534,6 @@
     loads.append(pltpu.make_async_copy(up_hbm, up_all, load_sem.at[6]))
     for load in loads:
         load.start()
-    entry_all = up_all.at[:, 0 : 3 * D]
-    late_load = pltpu.make_async_copy(entry_hbm, entry_all, load_sem.at[7])
 
     barrier = pltpu.get_barrier_semaphore()
     for step in range(1, NSEQ):
@@ -577,29 +577,31 @@
 
     pl.semaphore_wait(barrier, NSEQ - 1 + NGRP - 1)
 
-    sends = []
-
-    def start_when(cond, copy):
-        @pl.when(cond)
-        def _():
-            copy.start()
-
-        sends.append((cond, copy))
-
-    for d in range(1, chips):
-        up_to = lax.rem(s + 2 * d, NSEQ)
-        start_when(
-            chip + d < chips,
-            to_seq(up_to, kv.at[s], kv.at[s], kv_ssem.at[d - 1], kv_rsem.at[s]),
-        )
-    start_when(core == 0, to_seq(sib, kv.at[s], kv.at[s], kv_ssem.at[3], kv_rsem.at[s]))
-    for d in range(1, chips):
-        down_to = lax.rem(s - 2 * d + NSEQ, NSEQ)
-        start_when(
-            chip - d >= 0,
-            to_seq(down_to, qb.at[s], qb.at[s], q_ssem.at[d - 1], q_rsem.at[s]),
-        )
-    start_when(core == 1, to_seq(sib, qb.at[s], qb.at[s], q_ssem.at[3], q_rsem.at[s]))
+    launched = {}
+
+    def launch(name, copies):
+        for cond, copy in copies():
+            pl.when(cond)(copy.start)
+        launched[name] = copies
+
+    always = core >= 0
+
+    def spread(name, buffer, ssem, rsem, upward):
+        def copies():
+            found = []
+            for d in range(1, chips):
+                peer = lax.rem(s + (2 * d if upward else NSEQ - 2 * d), NSEQ)
+                cond = chip + d < chips if upward else chip >= d
+                found.append(
+                    (cond, to_seq(peer, buffer.at[s], buffer.at[s], ssem.at[d - 1], rsem.at[s]))
+                )
+            found.append((always, to_seq(sib, buffer.at[s], buffer.at[s], ssem.at[3], rsem.at[s])))
+            return found
+
+        launch(name, copies)
+
+    spread("kv", kv, kv_ssem, kv_rsem, True)
+    spread("q", qb, q_ssem, q_rsem, False)
 
     lane128 = lane_ids(LANES)
     rate_row = jnp.ones((1, LANES), F32)
@@ -621,23 +623,162 @@
 
     own_segment = segment_of(s)
 
-    def build_mask(i, carry):
-        b = i // 3
-        h = i - 3 * b
-        same = jnp.where(segment_of(b) == own_segment, 1.0, 0.0)
-        count = dot_nt((member[h].astype(F32) * same).astype(BF16), member[h])
-        masks[b, h] = count.astype(BF16)
-
-        @pl.when(b == s)
+    pair_width = 2 * T
+
+    def pair_lanes(cc):
+        return pl.ds(pl.multiple_of(cc * pair_width, LANES), pair_width)
+
+    def build_mask(cc, carry):
+        for h in range(3):
+            blocks = []
+            for i in range(2):
+                same = jnp.where(segment_of(2 * cc + i) == own_segment, 1.0, 0.0)
+                blocks.append((member[h].astype(F32) * same).astype(BF16))
+            count = dot_nt(member[h], jnp.concatenate(blocks, axis=0))
+            masks[h, :, pair_lanes(cc)] = count.astype(BF16)
+        return carry
+
+    lax.fori_loop(0, chips, build_mask, 0)
+    own_id = lax.broadcasted_iota(jnp.int32, (T, pair_width), 0) + core * T
+    pair_id = lax.broadcasted_iota(jnp.int32, (T, pair_width), 1)
+    own_block = (pair_id >= core * T) & (pair_id < core * T + T)
+    for h in range(3):
+        count = masks[h, :, pair_lanes(chip)].astype(F32) + jnp.where(own_block, 1.0, 0.0)
+        masks[h, :, pair_lanes(chip)] = jnp.where(pair_id <= own_id, count, 0.0).astype(BF16)
+        masks[h, :, pair_lanes(chips)] = jnp.where(own_id <= pair_id, count, 0.0).astype(BF16)
+
+    half = T // 2
+    width = part + 64
+    piece = D // NSEQ
+
+    def pack_half(tile, high):
+        top, bottom = tile[0:half], tile[half:T]
+        if high:
+            return join_halves(swap_halves(top), bottom).astype(BF16)
+        return join_halves(top, swap_halves(bottom)).astype(BF16)
+
+    right, left = lax.rem(g + 1, NGRP), lax.rem(g + NGRP - 1, NGRP)
+
+    def chain_start(name, at, ssem, rsem):
+        launch(
+            name + "0",
+            lambda: [
+                (g + 1 < NGRP, to_grp(right, at(g), at(g), ssem().at[0, 0], rsem().at[g])),
+                (g >= 1, to_grp(left, at(g), at(g), ssem().at[0, 1], rsem().at[g])),
+            ],
+        )
+
+    def chain_step(d, name, at, ssem, rsem):
+        def slots():
+            return lax.rem(g - d + NGRP, NGRP), lax.rem(g + d, NGRP)
+
+        def copies():
+            lower, upper = slots()
+            return [
+                (
+                    (g - d >= 0) & (g + 1 < NGRP),
+                    to_grp(right, at(lower), at(lower), ssem().at[d, 0], rsem().at[lower]),
+                ),
+                (
+                    (g + d < NGRP) & (g >= 1),
+                    to_grp(left, at(upper), at(upper), ssem().at[d, 1], rsem().at[upper]),
+                ),
+            ]
+
+        lower, upper = slots()
+        pl.when(g - d >= 0)(
+            to_grp(right, at(lower), at(lower), ssem().at[0, 0], rsem().at[lower]).wait_recv
+        )
+        pl.when(g + d < NGRP)(
+            to_grp(left, at(upper), at(upper), ssem().at[0, 1], rsem().at[upper]).wait_recv
+        )
+        if d < NGRP - 1:
+            launch(name + str(d), copies)
+
+    def direct_start(name, at, ssem, rsem):
+        def copies():
+            found = []
+            for step in range(1, NGRP):
+                peer = lax.rem(g + step, NGRP)
+                found.append((always, to_grp(peer, at(g), at(g), ssem.at[step - 1], rsem.at[g])))
+            return found
+
+        launch(name, copies)
+
+    def direct_wait(name, at, ssem, rsem):
+        for step in range(1, NGRP):
+            slot = lax.rem(g + step, NGRP)
+            to_grp(slot, at(slot), at(slot), ssem.at[0], rsem.at[slot]).wait_recv()
+
+    acc_a[...] = jnp.zeros_like(acc_a)
+    shift[...] = jnp.zeros_like(shift)
+
+    def pair_of(ref, cc, first, last):
+        return ref[pl.ds(2 * cc, 2), :, first:last].reshape(pair_width, last - first)
+
+    def weights_of(score, count):
+        count = count.astype(F32)
+        return jnp.where(count > 0.5, jnp.exp2(score * exp_scale) * count, 0.0)
+
+    def wait_pair(buffer, ssem, rsem, j, cc):
+        mine, other = 2 * cc + core, 2 * cc + 1 - core
+
+        @pl.when(j > 0)
         def _():
-            row_id = lax.broadcasted_iota(jnp.int32, (T, T), 0)
-            col_id = lax.broadcasted_iota(jnp.int32, (T, T), 1)
-            masks[b, h] = jnp.where(col_id <= row_id, count + 1.0, 0.0).astype(BF16)
-            masks[NSEQ, h] = jnp.where(row_id <= col_id, count + 1.0, 0.0).astype(BF16)
-
+            to_seq(sib, buffer.at[mine], buffer.at[mine], ssem.at[0], rsem.at[mine]).wait_recv()
+            to_seq(sib, buffer.at[mine], buffer.at[mine], ssem.at[3 + j], rsem.at[mine]).start()
+
+        to_seq(sib, buffer.at[other], buffer.at[other], ssem.at[0], rsem.at[other]).wait_recv()
+
+    def forward_step(j, carry):
+        cc = chip - j
+        wait_pair(kv, kv_ssem, kv_rsem, j, cc)
+        keys = pair_of(kv, cc, 0, 256)
+        values = pair_of(kv, cc, 128, 384)
+        for h in range(3):
+            weight = weights_of(dot_nt(qmask[h], keys), masks[h, :, pair_lanes(cc)])
+            row_sum = weight[:, 0:LANES]
+            for i in range(1, pair_width // LANES):
+                row_sum = row_sum + weight[:, LANES * i : LANES * i + LANES]
+            shift[h] += row_sum
+            low_weight = weight.astype(BF16)
+            masks[h, :, pair_lanes(cc)] = low_weight
+            acc_a[...] += dot_nn(low_weight, values) * slot_mask(h + 1)
         return carry
 
-    lax.fori_loop(0, 3 * NSEQ, build_mask, 0)
+    lax.fori_loop(0, chip + 1, forward_step, 0)
+    inverse = jnp.zeros((T, 256), F32)
+    for h in range(3):
+        inverse += slot_mask(h + 1) / jnp.sum(shift[h], axis=1, keepdims=True)
+    att_own = acc_a[...] * inverse
+    invden[...] = inverse
+    att[...] = att_own
+    for h in range(3):
+        tile = att_own[:, 0:128] if h == 0 else att_own[:, 128:256]
+        zmix[g, h] = pack_half(tile, h != 1)
+    mixed_gather = ("mixed", lambda i: zmix.at[i], zm_ssem, zm_rsem)
+    direct_start(*mixed_gather)
+
+    for d in range(1, chips):
+
+        @pl.when(chip + d < chips)
+        def _(d=d):
+            slot = lax.rem(s + 2 * d, NSEQ)
+            to_seq(sib, qb.at[slot], qb.at[slot], q_ssem.at[0], q_rsem.at[slot]).wait_recv()
+
+    def hand_on(buffer, ssem, rsem, upward):
+        found = []
+        for d in range(1, chips):
+            slot = lax.rem(s + (NSEQ - 2 * d if upward else 2 * d), NSEQ)
+            cond = chip >= d if upward else chip + d < chips
+            found.append(
+                (cond, to_seq(sib, buffer.at[slot], buffer.at[slot], ssem.at[3 + d], rsem.at[slot]))
+            )
+        return found
+
+    launch("q on", lambda: hand_on(qb, q_ssem, q_rsem, False))
+    launched["kv on"] = lambda: hand_on(kv, kv_ssem, kv_rsem, True)
+    launched["do on"] = lambda: hand_on(dob, do_ssem, do_rsem, False)
 
     loads[3].wait()
 
@@ -647,125 +788,14 @@
         return carry
 
     lax.fori_loop(0, FF // T, cot_times_down, 0)
-
-    acc_a[...] = jnp.zeros_like(acc_a)
-    den = shift
-    den[...] = jnp.zeros_like(den)
-
-    def forward_step(j, carry):
-        jj = j - 1 - core
-        d = jj // 2 + 1
-        which = jj % 2
-        far = jnp.where(which == 0, s - 2 * d, sib - 2 * d)
-        b = jnp.where(j == 0, s, jnp.where(jj < 0, s - 1, far))
-
-        @pl.when(j > 0)
-        def _():
-            to_seq(sib, kv.at[b], kv.at[b], kv_ssem.at[0], kv_rsem.at[b]).wait_recv()
-
-        @pl.when((jj >= 0) & (which == 0))
-        def _():
-            to_seq(sib, kv.at[b], kv.at[b], kv_ssem.at[3 + d], kv_rsem.at[b]).start()
-
-        for h in range(3):
-            score = dot_nt(qmask[h], kv[b, :, 0:256])
-            weight = jnp.exp2(score * exp_scale) * masks[b, h].astype(F32)
-            den[h] += weight[:, 0:128] + weight[:, 128:256] + weight[:, 256:384]
-            low_weight = weight.astype(BF16)
-            masks[b, h] = low_weight
-            acc_a[...] += dot_nn(low_weight, kv[b, :, 128:384]) * slot_mask(h + 1)
-        return carry
-
-    lax.fori_loop(0, s + 1, forward_step, 0)
-
-    inv_all = jnp.zeros((T, 256), F32)
-    for h in range(3):
-        inv_all = jnp.where(
-            slot_mask(h + 1) > 0.5, 1.0 / jnp.sum(den[h], axis=1, keepdims=True), inv_all
-        )
-    invden[...] = inv_all
-    att_own = acc_a[...] * inv_all
-    att[...] = att_own
-
-    def pack(target, tile_low, tile_high):
-        target[0:T, :] = tile_high.astype(BF16)
-        half = T // 2
-        target[T : T + half, :] = join_halves(
-            swap_halves(tile_low[half:T]), tile_low[0:half]
-        ).astype(BF16)
-
-    def unpack_pair(first, second, place):
-        half = T // 2
-        a_high = first[0:T, :].astype(F32)
-        a_rest = first[T : T + half, :].astype(F32)
-        b_high = second[0:T, :].astype(F32)
-        b_rest = second[T : T + half, :].astype(F32)
-        place(2, slice(0, T), b_high)
-        swapped = swap_halves(a_high)
-        place(0, slice(0, half), join_halves(swap_halves(a_rest), swapped[0:half]))
-        place(0, slice(half, T), join_halves(a_rest, swapped[half:T]))
-        place(1, slice(0, half), join_halves(swapped[0:half], b_rest))
-        place(1, slice(half, T), join_halves(swapped[half:T], swap_halves(b_rest)))
-
-    def chain_start(at, ssem, rsem):
-        start_when(g + 1 < NGRP, to_grp(lax.rem(g + 1, NGRP), at(g), at(g), ssem.at[0, 0], rsem.at[g]))
-        start_when(
-            g >= 1, to_grp(lax.rem(g + NGRP - 1, NGRP), at(g), at(g), ssem.at[0, 1], rsem.at[g])
-        )
-
-    def chain_step(d, at, ssem, rsem):
-        right = lax.rem(g + 1, NGRP)
-        left = lax.rem(g + NGRP - 1, NGRP)
-        lower = lax.rem(g - d + NGRP, NGRP)
-        upper = lax.rem(g + d, NGRP)
-
-        @pl.when(g - d >= 0)
-        def _():
-            to_grp(right, at(lower), at(lower), ssem.at[0, 0], rsem.at[lower]).wait_recv()
-
-        if d < NGRP - 1:
-            start_when(
-                (g - d >= 0) & (g + 1 < NGRP),
-                to_grp(right, at(lower), at(lower), ssem.at[d, 0], rsem.at[lower]),
-            )
-
-        @pl.when(g + d < NGRP)
-        def _():
-            to_grp(left, at(upper), at(upper), ssem.at[0, 1], rsem.at[upper]).wait_recv()
-
-        if d < NGRP - 1:
-            start_when(
-                (g + d < NGRP) & (g >= 1),
-                to_grp(left, at(upper), at(upper), ssem.at[d, 1], rsem.at[upper]),
-            )
-
-    pack(zmix.at[g], att_own[:, 0:128], att_own[:, 128:256])
-    chain_start(lambda i: zmix.at[i], zm_ssem, zm_rsem)
-
-    for d in range(1, chips):
-        slot = lax.rem(s + 2 * d, NSEQ)
-
-        @pl.when(chip + d < chips)
-        def _():
-            to_seq(sib, qb.at[slot], qb.at[slot], q_ssem.at[0], q_rsem.at[slot]).wait_recv()
-
-        start_when(
-            chip + d < chips,
-            to_seq(sib, qb.at[slot], qb.at[slot], q_ssem.at[3 + d], q_rsem.at[slot]),
-        )
-
-    for d in range(1, NGRP):
-        chain_step(d, lambda i: zmix.at[i], zm_ssem, zm_rsem)
-
-    def place_mixed(pair):
-        def place(tile, at, value):
-            first = pair * 2 * part + tile * LANES
-            mixed[at, first : first + LANES] = value.astype(BF16)
-
-        return place
-
-    for pair in range(NGRP // 2):
-        unpack_pair(zmix.at[2 * pair], zmix.at[2 * pair + 1], place_mixed(pair))
+    direct_wait(*mixed_gather)
+    for tile in range(D // LANES):
+        (g_a, h_a), (g_b, h_b) = divmod(2 * tile, 3), divmod(2 * tile + 1, 3)
+        first_head = zmix[g_a, h_a].astype(F32)
+        second_head = zmix[g_b, h_b].astype(F32)
+        cols = slice(tile * LANES, tile * LANES + LANES)
+        mixed[0:half, cols] = join_halves(first_head, swap_halves(second_head)).astype(BF16)
+        mixed[half:T, cols] = join_halves(swap_halves(first_head), second_head).astype(BF16)
 
     loads[4].wait()
     middle[...] = tok_ref[...].astype(F32) + dot_nn(mixed[...], exit_all[...])
@@ -776,43 +806,128 @@
         centered = value - jnp.mean(value, axis=1, keepdims=True)
         inverse = lax.rsqrt(jnp.mean(centered * centered, axis=1, keepdims=True) + EPS)
         plain = centered * inverse
-        plain2[at, :] = plain
-        inv2[at, :] = jnp.broadcast_to(inverse, (rows, LANES))
         n2[at, :] = (plain * gain2 + bias2).astype(BF16)
         return carry
 
     lax.fori_loop(0, T // rows, norm_two, 0)
 
+    def reduce_start(i, pieces, first_in, cond=None, tag=""):
+        launch(
+            f"first{i}{tag}",
+            lambda: [
+                (
+                    always if cond is None else cond(),
+                    to_seq(sib, pieces.at[1 - core], first_in, rs_s1.at[i], rs_r1.at[i]),
+                )
+            ],
+        )
+
+    def reduce_pass(i, pieces, first_in, second_in, cond=None, tag=""):
+        def given():
+            return always if cond is None else cond()
+
+        @pl.when(given())
+        def _():
+            to_seq(sib, pieces.at[core], first_in, rs_s1.at[i], rs_r1.at[i]).wait_recv()
+            for cc in range(chips):
+                pieces[core, cc] = (
+                    pieces[core, cc].astype(F32) + first_in[cc].astype(F32)
+                ).astype(BF16)
+
+        def copies():
+            found = []
+            for d in range(1, chips):
+                to_chip = lax.rem(chip + d, chips)
+                copy = to_seq(
+                    2 * to_chip + core,
+                    pieces.at[core, to_chip],
+                    second_in.at[chip],
+                    rs_s2.at[i, d - 1],
+                    rs_r2.at[i, chip],
+                )
+                found.append((given(), copy))
+            return found
+
+        launch(f"second{i}{tag}", copies)
+
+    def weight_gather(i, gathered):
+        return ("weight" + str(i), lambda j: gathered.at[j], lambda: rs_zs.at[i], lambda: rs_zr.at[i])
+
+    def reduce_end(i, pieces, second_in, gathered):
+        result = pieces[core, chip].astype(F32)
+        for d in range(1, chips):
+            slot = lax.rem(chip + d, chips)
+            to_seq(
+                sib, second_in.at[slot], second_in.at[slot], rs_s1.at[i], rs_r2.at[i, slot]
+            ).wait_recv()
+            result = result + second_in[slot].astype(F32)
+        gathered[g] = result.astype(BF16)
+        chain_start(*weight_gather(i, gathered))
+
     loads[6].wait()
-    gn2[...] = jnp.zeros_like(gn2)
+    cot_turned = jnp.transpose(
+        cot_ref[:, pl.ds(pl.multiple_of(lax.rem(g, 3) * width, LANES), width)].astype(F32)
+    ).astype(BF16)
 
     def feed_forward(i, carry):
-        at = pl.ds(pl.multiple_of(i * T, T), T)
+        c = lax.rem(g + i, NGRP)
+        at = pl.ds(pl.multiple_of(c * D, LANES), D)
         hidden = dot_nn(n2[...], up_all[:, at])
         cdf = 0.5 + 0.5 * lax.erf(hidden * (0.5**0.5))
-        active[:, at] = (hidden * cdf).astype(BF16)
+        low_active = (hidden * cdf).astype(BF16)
+        active[:, at] = low_active
         density = jnp.exp2(hidden * hidden * (-0.5 * LOG2E)) * 0.3989422804014327
-        low_grad = (ghid[:, at].astype(F32) * (cdf + hidden * density)).astype(BF16)
-        ghid[:, at] = low_grad
-        gn2[...] += dot_nt(low_grad, up_all[:, at])
+        ghid[:, at] = (ghid[:, at].astype(F32) * (cdf + hidden * density)).astype(BF16)
+
+        @pl.when(g < 3)
+        def _():
+            turned = dot_nn(cot_turned, active[:, at]).astype(BF16)
+            pc_down[0, c] = turned[:, 0:T]
+            pc_down[1, c] = turned[:, T : 2 * T]
+
+        @pl.when(i == 0)
+        def _():
+            for j in range(2):
+                up_grad = dot_tn(n2[...], ghid[:, pl.ds(pl.multiple_of(g * D + T * j, LANES), T)])
+                for t in range(NSEQ):
+                    pc_up[t % 2, t // 2, :, T * j : T * j + T] = up_grad[
+                        piece * t : piece * t + piece, :
+                    ].astype(BF16)
+            reduce_start(0, pc_up, r1_up)
+
+        @pl.when(i == 1)
+        def _():
+            reduce_pass(0, pc_up, r1_up, r2_up)
+
         return carry
 
-    lax.fori_loop(0, FF // T, feed_forward, 0)
-    late_load.start()
+    lax.fori_loop(0, NGRP, feed_forward, 0)
+    reduce_start(1, pc_down, r1_down, lambda: g < 3, "down")
+
+    def back_through_up(i, carry):
+        at = pl.ds(pl.multiple_of(i * 256, 256), 256)
+        gn2[:, at] = dot_nt(ghid[...], up_all[at, :])
+        return carry
+
+    lax.fori_loop(0, D // 256, back_through_up, 0)
+    reduce_pass(1, pc_down, r1_down, r2_down, lambda: g < 3, "down")
 
     stat[s] = jnp.zeros((8, D), F32)
 
     def norm_two_back(i, carry):
         at = pl.ds(pl.multiple_of(i * rows, rows), rows)
         upstream = gn2[at, :]
-        plain = plain2[at, :]
+        value = middle[at, :]
+        centered = value - jnp.mean(value, axis=1, keepdims=True)
+        inverse = lax.rsqrt(jnp.mean(centered * centered, axis=1, keepdims=True) + EPS)
+        plain = centered * inverse
         scaled = upstream * gain2
         inner = (
             scaled
             - jnp.mean(scaled, axis=1, keepdims=True)
             - plain * jnp.mean(scaled * plain, axis=1, keepdims=True)
         )
-        grad = cot_ref[at, :].astype(F32) + inv2[at, 0:1] * inner
+        grad = cot_ref[at, :].astype(F32) + inverse * inner
         gmid[at, :] = grad
         gbranch[at, :] = grad.astype(BF16)
         stat[s, 0:1, :] += jnp.sum(upstream * plain, axis=0, keepdims=True)
@@ -834,238 +949,154 @@
         numer_grad = jnp.where(lane256 == 2 * h + 1, low, numer_grad)
     dob[s] = numer_grad.astype(BF16)
 
-    for d in range(1, chips):
-        down_to = lax.rem(s - 2 * d + NSEQ, NSEQ)
-        start_when(
-            chip - d >= 0,
-            to_seq(down_to, dob.at[s], dob.at[s], do_ssem.at[d - 1], do_rsem.at[s]),
-        )
-    start_when(core == 1, to_seq(sib, dob.at[s], dob.at[s], do_ssem.at[3], do_rsem.at[s]))
-
-    width = part + 64
-    up_grad = dot_tn(n2[...], ghid[:, pl.ds(pl.multiple_of(g * D, LANES), D)])
-    for t in range(NSEQ):
-        pc_up[t % 2, t // 2] = up_grad[96 * t : 96 * t + 96, :].astype(BF16)
-
-    @pl.when(g < 3)
-    def _():
-        cols = pl.ds(pl.multiple_of(lax.rem(g, 3) * width, LANES), width)
-
-        def down_piece(t, carry):
-            at = pl.ds(pl.multiple_of(t * T, T), T)
-            pc_down[t % 2, t // 2] = dot_tn(active[:, at], cot_ref[:, cols]).astype(BF16)
-            return carry
-
-        lax.fori_loop(0, NSEQ, down_piece, 0)
+    spread("do", dob, do_ssem, do_rsem, False)
+
+    reduce_end(0, pc_up, r2_up, ag_up)
 
     @pl.when(g == 3)
     def _():
         exit_grad = dot_tn(mixed[...], gbranch[...]).astype(BF16)
         for t in range(NSEQ):
-            for i in range(3):
-                pc_down[t % 2, t // 2, 96 * i : 96 * i + 96, :] = exit_grad[
-                    96 * t : 96 * t + 96, width * i : width * i + width
+            for i in range(2):
+                pc_down[t % 2, t // 2, piece * i : piece * i + piece, :] = exit_grad[
+                    piece * t : piece * t + piece, T * i : T * i + T
                 ]
-            pc_down[t % 2, t // 2, 288:384, :] = jnp.zeros((96, width), BF16)
-
-    def reduce_start(i, pieces, first_in):
-        start_when(
-            core >= 0,
-            to_seq(sib, pieces.at[1 - core], first_in, rs_s1.at[i], rs_r1.at[i]),
-        )
-
-    def reduce_pass(i, pieces, first_in, total, second_in):
-        to_seq(sib, pieces.at[core], first_in, rs_s1.at[i], rs_r1.at[i]).wait_recv()
-        for cc in range(chips):
-            total[cc] = (pieces[core, cc].astype(F32) + first_in[cc].astype(F32)).astype(BF16)
-        for d in range(1, chips):
-            to_chip = lax.rem(chip + d, chips)
-            start_when(
-                core >= 0,
-                to_seq(
-                    2 * to_chip + core,
-                    total.at[to_chip],
-                    second_in.at[chip],
-                    rs_s2.at[i, d - 1],
-                    rs_r2.at[i, chip],
-                ),
-            )
-
-    def reduce_end(i, total, second_in, gathered):
-        result = total[chip].astype(F32)
-        for d in range(1, chips):
-            slot = lax.rem(chip + d, chips)
-            to_seq(
-                sib, second_in.at[slot], second_in.at[slot], rs_s1.at[i], rs_r2.at[i, slot]
-            ).wait_recv()
-            result = result + second_in[slot].astype(F32)
-        gathered[g] = result.astype(BF16)
-        chain_start(lambda j: gathered.at[j], rs_zs.at[i], rs_zr.at[i])
-
-    reduce_start(0, pc_up, r1_up)
-    reduce_start(1, pc_down, r1_down)
+            pc_down[t % 2, t // 2, 2 * piece : width, :] = jnp.zeros((width - 2 * piece, T), BF16)
+
+    reduce_start(1, pc_down, r1_down, lambda: g == 3, "exit")
+    reduce_pass(1, pc_down, r1_down, r2_down, lambda: g == 3, "exit")
 
     for h in range(3):
         qmask[h] = (dob[s].astype(F32) * slot_mask(h + 1)).astype(BF16)
     acc_a[...] = jnp.zeros_like(acc_a)
 
-    def query_side(b, carry):
+    def query_side(cc, carry):
+        keys = pair_of(kv, cc, 0, 256)
+        values = pair_of(kv, cc, 128, 384)
         for h in range(3):
-            pressure = dot_nt(qmask[h], kv[b, :, 128:384])
-            row_shift = shift[h]
-            row_shift = jnp.concatenate([row_shift, row_shift, row_shift], axis=1)
-            slope = (masks[b, h].astype(F32) * (pressure - row_shift)).astype(BF16)
-            acc_a[...] += dot_nn(slope, kv[b, :, 0:256]) * slot_mask(h)
+            row_shift = jnp.concatenate([shift[h]] * (pair_width // LANES), axis=1)
+            pressure = dot_nt(qmask[h], values) - row_shift
+            slope = (masks[h, :, pair_lanes(cc)].astype(F32) * pressure).astype(BF16)
+            acc_a[...] += dot_nn(slope, keys) * slot_mask(h)
         return carry
 
-    lax.fori_loop(0, s + 1, query_side, 0)
-    dq = pltpu.roll(acc_a[...] * scale, 64, axis=1)
-    pack(zdq.at[g], dq[:, 0:128], dq[:, 128:256])
-    chain_start(lambda i: zdq.at[i], zq_ssem, zq_rsem)
-
-    reduce_pass(0, pc_up, r1_up, y_up, r2_up)
-    reduce_pass(1, pc_down, r1_down, y_down, r2_down)
-
-    acc_b[...] = jnp.zeros_like(acc_b)
-    acc_c[...] = jnp.zeros_like(acc_c)
+    lax.fori_loop(0, chip + 1, query_side, 0)
+    dq = acc_a[...] * scale
+
+    def weight_pieces(pieces, grad):
+        for t in range(NSEQ):
+            pieces[t % 2, t // 2] = grad[piece * t : piece * t + piece, :].astype(BF16)
+
+    weight_pieces(pc_eq, dot_tn(n1[...], dq.astype(BF16)))
+    reduce_start(2, pc_eq, r1_eq)
+    chain_step(1, *weight_gather(0, ag_up))
+
     v_tile = kv[s, :, 128:384].astype(F32)
     k_tile = kv[s, :, 0:256].astype(F32)
     for h in range(3):
         qmask[h] = (k_tile * slot_mask(h)).astype(BF16)
         minus = jnp.where((lane256 == 2 * h) | (lane256 == 2 * h + 1), -1.0, 0.0)
         qmask[3 + h] = (v_tile * slot_mask(h + 1) + minus).astype(BF16)
+    acc_b[...] = jnp.zeros_like(acc_b)
+    acc_c[...] = jnp.zeros_like(acc_c)
 
     def key_side(j, carry):
-        jj = j - 2 + core
-        d = jj // 2 + 1
-        which = jj % 2
-        far = jnp.where(which == 0, s + 2 * d, sib + 2 * d)
-        b = jnp.where(j == 0, s, jnp.where(jj < 0, s + 1, far))
-
-        @pl.when(j > 0)
+        cc = chip + j
+        wait_pair(dob, do_ssem, do_rsem, j, cc)
+        other = 2 * cc + 1 - core
+        to_seq(sib, qb.at[other], qb.at[other], q_ssem.at[0], q_rsem.at[other]).wait_recv()
+        queries = pair_of(qb, cc, 0, 256)
+        grads = pair_of(dob, cc, 0, 256)
+        for h in range(3):
+            count = masks[h, :, pair_lanes(jnp.where(j == 0, chips, cc))]
+            weight = weights_of(dot_nt(qmask[h], queries), count)
+            slope = (weight * dot_nt(qmask[3 + h], grads)).astype(BF16)
+            acc_b[...] += dot_nn(slope, queries) * slot_mask(h)
+            acc_c[...] += dot_nn(weight.astype(BF16), grads) * slot_mask(h + 1)
+
+        @pl.when(j == 0)
         def _():
-            to_seq(sib, dob.at[b], dob.at[b], do_ssem.at[0], do_rsem.at[b]).wait_recv()
-
-        @pl.when((jj >= 0) & (which == 0))
+            reduce_pass(2, pc_eq, r1_eq, r2_eq)
+            chain_step(2, *weight_gather(0, ag_up))
+
+        @pl.when((j == 1) | ((j == 0) & (chip == chips - 1)))
         def _():
-            to_seq(sib, dob.at[b], dob.at[b], do_ssem.at[3 + d], do_rsem.at[b]).start()
-
-        @pl.when((j > 0) & ((jj < 0) | (which == 1)))
-        def _():
-            to_seq(sib, qb.at[b], qb.at[b], q_ssem.at[0], q_rsem.at[b]).wait_recv()
-
-        at = jnp.where(j == 0, NSEQ, b)
-        for h in range(3):
-            score = dot_nt(qmask[h], qb[b])
-            weight = jnp.exp2(score * exp_scale) * masks[at, h].astype(F32)
-            pressure = dot_nt(qmask[3 + h], dob[b])
-            slope = (weight * pressure).astype(BF16)
-            acc_b[...] += dot_nn(slope, qb[b]) * slot_mask(h)
-            acc_c[...] += dot_nn(weight.astype(BF16), dob[b]) * slot_mask(h + 1)
+            reduce_end(1, pc_down, r2_down, ag_down)
+
         return carry
 
-    lax.fori_loop(0, NSEQ - s, key_side, 0)
-
-    dk = pltpu.roll(acc_b[...] * scale, 64, axis=1)
-    pack(zdkv.at[g, 0], dk[:, 0:128], dk[:, 128:256])
-    dv = acc_c[...]
-    pack(zdkv.at[g, 1], dv[:, 0:128], dv[:, 128:256])
-    chain_start(lambda i: zdkv.at[i], zk_ssem, zk_rsem)
-
-    dfull = ghid.at[:, 0 : 3 * D]
-    dpack = ghid.at[:, 3 * D : 3 * D + 640]
-    dpack[:, 0:128] = join_halves(swap_halves(dq[:, 0:128]), swap_halves(dq[:, 128:256])).astype(BF16)
-    dpack[:, 128:256] = join_halves(swap_halves(dq[:, 128:256]), dk[:, 0:128]).astype(BF16)
-    dpack[:, 256:384] = dk[:, 128:256].astype(BF16)
-    dpack[:, 384:512] = join_halves(swap_halves(dv[:, 0:128]), swap_halves(dv[:, 128:256])).astype(BF16)
-    dpack[:, 512:640] = join_halves(swap_halves(dv[:, 128:256]), jnp.zeros((T, LANES), F32)).astype(BF16)
-    entry_grad = dot_tn(n1[...], dpack[...])
-    for t in range(NSEQ):
-        pc_entry[t % 2, t // 2] = entry_grad[96 * t : 96 * t + 96, :].astype(BF16)
-    reduce_start(2, pc_entry, r1_entry)
-
-    reduce_end(0, y_up, r2_up, ag_up)
-    reduce_end(1, y_down, r2_down, ag_down)
-    for d in range(1, NGRP):
-        chain_step(d, lambda i: zdq.at[i], zq_ssem, zq_rsem)
-    reduce_pass(2, pc_entry, r1_entry, y_entry, r2_entry)
-    for d in range(1, NGRP):
-        chain_step(d, lambda i: zdkv.at[i], zk_ssem, zk_rsem)
-
-    def place_grad(first_col):
-        def place(tile, at, value):
-            first = first_col + tile * LANES
-            dfull[at, first : first + LANES] = value.astype(BF16)
-
-        return place
-
-    for pair in range(NGRP // 2):
-        first_col = pair * 2 * part
-        unpack_pair(zdq.at[2 * pair], zdq.at[2 * pair + 1], place_grad(first_col))
-        for t in range(2):
-            unpack_pair(
-                zdkv.at[2 * pair, t], zdkv.at[2 * pair + 1, t], place_grad((t + 1) * D + first_col)
-            )
-
-    out_ref[...] = (middle[...] + dot_nn(active[...], down_all[...])).astype(BF16)
-    reduce_end(2, y_entry, r2_entry, ag_entry)
-    late_load.wait()
-    gn2[...] = dot_nt(dfull[...], up_all[:, 0 : 3 * D])
-
-    def norm_one_back(i, carry):
-        at = pl.ds(pl.multiple_of(i * rows, rows), rows)
-        value = tok_ref[at, :].astype(F32)
-        centered = value - jnp.mean(value, axis=1, keepdims=True)
-        inverse = lax.rsqrt(jnp.mean(centered * centered, axis=1, keepdims=True) + EPS)
-        plain = centered * inverse
-        upstream = gn2[at, :]
-        scaled = upstream * gain1
-        inner = (
-            scaled
-            - jnp.mean(scaled, axis=1, keepdims=True)
-            - plain * jnp.mean(scaled * plain, axis=1, keepdims=True)
-        )
-        tgrad_ref[at, :] = (gmid[at, :] + inverse * inner).astype(BF16)
-        stat[s, 2:3, :] += jnp.sum(upstream * plain, axis=0, keepdims=True)
-        stat[s, 3:4, :] += jnp.sum(upstream, axis=0, keepdims=True)
+    lax.fori_loop(0, chips - chip, key_side, 0)
+
+    dk, dv = acc_b[...] * scale, acc_c[...]
+    part_sum = dot_nt(jnp.where(is_odd, pltpu.roll(dq, 64, axis=1), dq).astype(BF16), win[0])
+    part_sum += dot_nt(jnp.where(is_odd, pltpu.roll(dk, 64, axis=1), dk).astype(BF16), win[1])
+    part_sum += dot_nt(jnp.where(is_odd, dv, pltpu.roll(dv, 192, axis=1)).astype(BF16), win[2])
+    gn2[...] = part_sum
+    n2[...] = part_sum.astype(BF16)
+    own_rows = pl.ds(pl.multiple_of(g * piece, piece), piece)
+
+    def row_copies():
+        found = []
+        for step in range(1, NGRP):
+            peer = lax.rem(g + step, NGRP)
+            rows_of = pl.ds(pl.multiple_of(peer * piece, piece), piece)
+            copy = to_grp(peer, n2.at[rows_of, :], drecv.at[g], zd_ssem.at[step - 1], zd_rsem.at[g])
+            found.append((always, copy))
+        return found
+
+    launch("rows", row_copies)
+
+    dpack = ghid.at[:, 0:384]
+    dpack[:, 0:128] = dk[:, 0:128].astype(BF16)
+    dpack[:, 128:256] = join_halves(dk[:, 128:256], dv[:, 0:128]).astype(BF16)
+    dpack[:, 256:384] = dv[:, 128:256].astype(BF16)
+    weight_pieces(pc_ekv, dot_tn(n1[...], dpack[...]))
+    reduce_start(3, pc_ekv, r1_ekv)
+    chain_step(1, *weight_gather(1, ag_down))
+    reduce_end(2, pc_eq, r2_eq, ag_eq)
+
+    def through_down(i, carry):
+        at = pl.ds(pl.multiple_of(i * 256, 256), 256)
+        out_ref[:, at] = (middle[:, at] + dot_nn(active[...], down_all[:, at])).astype(BF16)
         return carry
 
-    lax.fori_loop(0, T // rows, norm_one_back, 0)
-    for step in range(1, NSEQ):
-        peer = lax.rem(s + step, NSEQ)
-        start_when(
-            core >= 0, to_seq(peer, stat.at[s], stat.at[s], st_ssem.at[step - 1], st_rsem.at[s])
-        )
-
-    for d in range(1, NGRP):
-        chain_step(d, lambda i: ag_up.at[i], rs_zs.at[0], rs_zr.at[0])
-    for i in range(NGRP):
-        oup_ref[:, D * i : D * i + D] = ag_up[i]
-    for d in range(1, NGRP):
-        chain_step(d, lambda i: ag_down.at[i], rs_zs.at[1], rs_zr.at[1])
-    for i in range(3):
-        odown_ref[:, width * i : width * i + width] = ag_down[i]
-        oexit_ref[:, width * i : width * i + width] = ag_down[3, 96 * i : 96 * i + 96, :]
-    for d in range(1, NGRP):
-        chain_step(d, lambda i: ag_entry.at[i], rs_zs.at[2], rs_zr.at[2])
-    for pair in range(NGRP // 2):
-        a = ag_entry[2 * pair].astype(F32)
-        b = ag_entry[2 * pair + 1].astype(F32)
-        first = pair * 2 * part
-        tiles = (
-            (0, a[:, 0:128]),
-            (1, join_halves(a[:, 128:256], swap_halves(b[:, 0:128]))),
-            (2, join_halves(swap_halves(b[:, 0:128]), swap_halves(b[:, 128:256]))),
-            (6, join_halves(swap_halves(a[:, 128:256]), swap_halves(a[:, 256:384]))),
-            (7, join_halves(swap_halves(a[:, 256:384]), b[:, 128:256])),
-            (8, b[:, 256:384]),
-            (12, a[:, 384:512]),
-            (13, join_halves(a[:, 512:640], swap_halves(b[:, 384:512]))),
-            (14, join_halves(swap_halves(b[:, 384:512]), swap_halves(b[:, 512:640]))),
-        )
-        for tile, value in tiles:
-            at = tile * LANES + first
-            oentry_ref[:, at : at + LANES] = value.astype(BF16)
+    lax.fori_loop(0, D // 256, through_down, 0)
+    reduce_pass(3, pc_ekv, r1_ekv, r2_ekv)
+    chain_step(2, *weight_gather(1, ag_down))
+    chain_step(1, *weight_gather(2, ag_eq))
+
+    upstream = gn2[own_rows, :]
+    for step in range(1, NGRP):
+        slot = lax.rem(g + step, NGRP)
+        to_grp(slot, drecv.at[slot], drecv.at[slot], zd_ssem.at[0], zd_rsem.at[slot]).wait_recv()
+        upstream = upstream + drecv[slot].astype(F32)
+    value = tok_ref[own_rows, :].astype(F32)
+    centered = value - jnp.mean(value, axis=1, keepdims=True)
+    inverse = lax.rsqrt(jnp.mean(centered * centered, axis=1, keepdims=True) + EPS)
+    plain = centered * inverse
+    scaled = upstream * gain1
+    inner = (
+        scaled
+        - jnp.mean(scaled, axis=1, keepdims=True)
+        - plain * jnp.mean(scaled * plain, axis=1, keepdims=True)
+    )
+    tz[g] = (gmid[own_rows, :] + inverse * inner).astype(BF16)
+    token_gather = ("token", lambda i: tz.at[i], zt_ssem, zt_rsem)
+    direct_start(*token_gather)
+    stat[s, 2:3, :] = jnp.sum(upstream * plain, axis=0, keepdims=True)
+    stat[s, 3:4, :] = jnp.sum(upstream, axis=0, keepdims=True)
+
+    def stat_copies():
+        found = []
+        for step in range(1, NSEQ):
+            peer = lax.rem(s + step, NSEQ)
+            copy = to_seq(peer, stat.at[s], stat.at[s], st_ssem.at[step - 1], st_rsem.at[s])
+            found.append((always, copy))
+        return found
+
+    launch("stat", stat_copies)
+    reduce_end(3, pc_ekv, r2_ekv, ag_ekv)
+    chain_step(2, *weight_gather(2, ag_eq))
 
     for step in range(1, NSEQ):
         slot = lax.rem(s + step, NSEQ)
@@ -1073,25 +1104,75 @@
     total_stat = stat[0]
     for i in range(1, NSEQ):
         total_stat = total_stat + stat[i]
-    ostat_ref[...] = total_stat
-
-    for cond, copy in sends:
-
-        @pl.when(cond)
-        def _(copy=copy):
-            copy.wait_send()
-
-    for d in range(1, chips):
-
-        @pl.when(chip - d >= 0)
-        def _(d=d):
-            slot = lax.rem(s - 2 * d + NSEQ, NSEQ)
-            to_seq(sib, kv.at[slot], kv.at[slot], kv_ssem.at[3 + d], kv_rsem.at[slot]).wait_send()
-
-        @pl.when(chip + d < chips)
-        def _(d=d):
-            slot = lax.rem(s + 2 * d, NSEQ)
-            to_seq(sib, dob.at[slot], dob.at[slot], do_ssem.at[3 + d], do_rsem.at[slot]).wait_send()
+    stat_z[g] = total_stat
+    direct_start("stat z", lambda i: stat_z.at[i], sz_ssem, sz_rsem)
+
+    chain_step(3, *weight_gather(0, ag_up))
+    chain_step(1, *weight_gather(3, ag_ekv))
+    for i in range(NGRP):
+        oup_ref[:, D * i : D * i + D] = ag_up[i]
+    chain_step(3, *weight_gather(1, ag_down))
+    chain_step(2, *weight_gather(3, ag_ekv))
+    for i in range(3):
+        odown_ref[:, width * i : width * i + width] = jnp.transpose(ag_down[i].astype(F32)).astype(BF16)
+    for i in range(2):
+        oexit_ref[:, T * i : T * i + T] = ag_down[3, piece * i : piece * i + piece, :]
+    chain_step(3, *weight_gather(2, ag_eq))
+
+    def place_entry(first, tiles):
+        for tile, value in enumerate(tiles):
+            at = first + tile * LANES
+            oentry_ref[:, at : at + LANES] = value.astype(BF16)
+
+    for pair in range(NGRP // 2):
+        a = ag_eq[2 * pair].astype(F32)
+        b = ag_eq[2 * pair + 1].astype(F32)
+        turned = swap_halves(b[:, 0:128])
+        place_entry(
+            pair * 2 * part,
+            (
+                a[:, 0:128],
+                join_halves(a[:, 128:256], turned),
+                join_halves(turned, swap_halves(b[:, 128:256])),
+            ),
+        )
+    direct_wait(*token_gather)
+    for i in range(NGRP):
+        tgrad_ref[piece * i : piece * i + piece, :] = tz[i]
+    total_stat = jnp.zeros((8, D), F32)
+    for step in range(1, NGRP):
+        slot = lax.rem(g + step, NGRP)
+        to_grp(slot, stat_z.at[slot], stat_z.at[slot], sz_ssem.at[0], sz_rsem.at[slot]).wait_recv()
+    for i in range(NGRP):
+        total_stat = total_stat + stat_z[i]
+    row_id = lax.broadcasted_iota(jnp.int32, (8, 1), 0)
+    ostat_ref[...] = jnp.where(row_id < 2, stat_z[g], total_stat)
+    chain_step(3, *weight_gather(3, ag_ekv))
+    for pair in range(NGRP // 2):
+        a = ag_ekv[2 * pair].astype(F32)
+        b = ag_ekv[2 * pair + 1].astype(F32)
+        turned = swap_halves(b[:, 0:128])
+        place_entry(
+            D + pair * 2 * part,
+            (
+                a[:, 0:128],
+                join_halves(a[:, 128:256], turned),
+                join_halves(turned, swap_halves(b[:, 128:256])),
+            ),
+        )
+        turned = swap_halves(a[:, 256:384])
+        place_entry(
+            2 * D + pair * 2 * part,
+            (
+                join_halves(swap_halves(a[:, 128:256]), turned),
+                join_halves(turned, b[:, 128:256]),
+                b[:, 256:384],
+            ),
+        )
+
+    for copies in launched.values():
+        for cond, copy in copies():
+            pl.when(cond)(copy.wait_send)
 
 
 def finish_kernel(
@@ -1183,7 +1264,7 @@
     NSEQ = seq_count
     chips = NSEQ // 2
     sizes = (T, D, HEADS, E, FF, NSEQ, NGRP)
-    share = T * 3 // 2
+    piece = D // NSEQ
     vmem = pl.BlockSpec(memory_space=pltpu.VMEM)
     smem = pl.BlockSpec(memory_space=pltpu.SMEM)
     anywhere = pl.BlockSpec(memory_space=pl.ANY)
@@ -1197,8 +1278,6 @@
         pltpu.VMEM((T, D), BF16),
         pltpu.VMEM((T, D), BF16),
         pltpu.VMEM((T, D), F32),
-        pltpu.VMEM((T, LANES), F32),
-        pltpu.VMEM((T, D), F32),
         pltpu.VMEM((T, D), F32),
         pltpu.VMEM((T, D), BF16),
         pltpu.VMEM((T, D), BF16),
@@ -1206,7 +1285,7 @@
         pltpu.VMEM((T, FF), BF16),
         pltpu.VMEM((T, D), F32),
         pltpu.VMEM((3, T, LANES), BF16),
-        pltpu.VMEM((NSEQ + 1, 3, T, T), BF16),
+        pltpu.VMEM((3, T, (NSEQ + 2) * T), BF16),
         pltpu.VMEM((NSEQ, T, 384), BF16),
         pltpu.VMEM((NSEQ, T, 256), BF16),
         pltpu.VMEM((NSEQ, T, 256), BF16),
@@ -1217,48 +1296,50 @@
         pltpu.VMEM((T, 256), F32),
         pltpu.VMEM((T, 256), F32),
         pltpu.VMEM((T, 256), F32),
-        pltpu.VMEM((NGRP, share, LANES), BF16),
-        pltpu.VMEM((NGRP, share, LANES), BF16),
-        pltpu.VMEM((NGRP, 2, share, LANES), BF16),
+        pltpu.VMEM((NGRP, 3, T // 2, LANES), BF16),
+        pltpu.VMEM((NGRP, piece, D), BF16),
+        pltpu.VMEM((NGRP, piece, D), BF16),
         pltpu.VMEM((NSEQ, 8, D), F32),
+        pltpu.VMEM((NGRP, 8, D), F32),
     ]
-    for rows, cols in ((T, 256), (96, D), (96, 640)):
+    for rows, cols in ((piece, D), (256, T), (piece, 256), (piece, 384)):
         scratch += [
             pltpu.VMEM((2, chips, rows, cols), BF16),
-            pltpu.VMEM((chips, rows, cols), BF16),
             pltpu.VMEM((chips, rows, cols), BF16),
             pltpu.VMEM((chips, rows, cols), BF16),
             pltpu.VMEM((NGRP, rows, cols), BF16),
         ]
     scratch += [
-        dma((8,)),
+        dma((7,)),
         dma((7,)),
         dma((NSEQ,)),
         dma((7,)),
         dma((NSEQ,)),
         dma((7,)),
         dma((NSEQ,)),
-        dma((3, 2)),
+        dma((NGRP - 1,)),
         dma((NGRP,)),
-        dma((3, 2)),
+        dma((NGRP - 1,)),
         dma((NGRP,)),
-        dma((3, 2)),
+        dma((NGRP - 1,)),
         dma((NGRP,)),
-        dma((3,)),
-        dma((3,)),
-        dma((3, 3)),
-        dma((3, chips)),
-        dma((3, 3, 2)),
-        dma((3, NGRP)),
+        dma((4,)),
+        dma((4,)),
+        dma((4, 3)),
+        dma((4, chips)),
+        dma((4, 3, 2)),
+        dma((4, NGRP)),
         dma((NSEQ - 1,)),
         dma((NSEQ,)),
+        dma((NGRP - 1,)),
+        dma((NGRP,)),
     ]
     out_shape = (
         jax.ShapeDtypeStruct((T, D), BF16),
         jax.ShapeDtypeStruct((T, D), BF16),
-        jax.ShapeDtypeStruct((96, 3 * D), BF16),
-        jax.ShapeDtypeStruct((96, D), BF16),
-        jax.ShapeDtypeStruct((96, FF), BF16),
+        jax.ShapeDtypeStruct((piece, 3 * D), BF16),
+        jax.ShapeDtypeStruct((piece, D), BF16),
+        jax.ShapeDtypeStruct((piece, FF), BF16),
         jax.ShapeDtypeStruct((T, D), BF16),
         jax.ShapeDtypeStruct((8, D), F32),
     )
@@ -1286,7 +1367,7 @@
         up_weight,
         down_weight,
     )
-    part = D // NSEQ
+    part = piece
     finish_shape = (
         jax.ShapeDtypeStruct((T, D), BF16),
         jax.ShapeDtypeStruct((T, D), BF16),

time: 130 us -> 126 us (0.969)
  Pallas kernels: 129 us -> 124 us
    pallas_call x1, Pallas kernels: 125 us -> 121 us  [fast_on_device(): pl.pallas_call(partial(layer_kernel, sizes), out_shape=out_shape, in_spec...]
where the time goes in v3:
time: 126 us; the launch traced here: 125 us
  Pallas kernels  124 us (98%)
    pallas_call x1, Pallas kernels, fast_on_device(): pl.pallas_call(partial(layer_kernel, sizes), out_shape=out_shape, in_spec...  121 us
    pallas_call x1, Pallas kernels, fast_on_device(): pl.pallas_call(finish_kernel, out_shape=finish_shape, in_specs=[anywhere]...  3.95 us

profile of v3, /device:TPU:0, one launch (start us, length us, event | category | flops | bytes accessed | tf_op | source)
XLA Modules:
  0.0 125.3 jit_solution(5161233896563099400)
XLA Ops:
  0.6 120.5 %layer.1 = (bf16[384,768]{1,0:T(8,128)(2,1)}, bf16[384,768]{1,0:T(8,128)(2,1)}, bf16[96,2304]{1,0:T(8,128)(2,1)}, bf16[96,768]{1,0:T(8,128)(2,1)}, bf16[96,3072]...) custom-call(s32[4]{0:T(128)} %dil_ref.1, s32[4,12]{1,0:T(4,128)} %off_ref.1, bf16[384,768]{1,0:T(8,128)(2,1)} %tok_ref.1, ...), custom_call_target="tpu_custom_call" | custom-call | tf_op jit(solution)/shard_map/layer/pallas_call | solution.py:1346
  121.2 4.0 %finish.1 = (bf16[384,768]{1,0:T(8,128)(2,1)}, bf16[384,768]{1,0:T(8,128)(2,1)}, f32[96,2304]{1,0:T(8,128)}, f32[96,768]{1,0:T(8,128)}, f32[96,3072]{1,0:T(8,128...) custom-call(bf16[384,768]{1,0:T(8,128)(2,1)} %get-tuple-element.17.out_in, ...), custom_call_target="tpu_custom_call" | custom-call | tf_op jit(solution)/shard_map/finish/pallas_call | solution.py:1379

commit v4 on v3

--- a/solution.py
+++ b/solution.py
@@ -410,7 +410,6 @@
     ostat_ref,
     win,
     exit_all,
-    exit_win,
     up_all,
     down_all,
     n1,
@@ -439,14 +438,14 @@
     tz,
     stat,
     stat_z,
+    r1_exit,
+    r2_exit,
+    r1_down,
+    r2_down,
     pc_up,
     r1_up,
     r2_up,
     ag_up,
-    pc_down,
-    r1_down,
-    r2_down,
-    ag_down,
     pc_eq,
     r1_eq,
     r2_eq,
@@ -524,15 +523,8 @@
         )
     loads.append(pltpu.make_async_copy(down_hbm, down_all, load_sem.at[3]))
     loads.append(pltpu.make_async_copy(exit_hbm, exit_all, load_sem.at[4]))
-    loads.append(
-        pltpu.make_async_copy(
-            exit_hbm.at[pl.ds(pl.multiple_of(part * g, 64), part), :],
-            exit_win.at[pl.ds(64, part), :],
-            load_sem.at[5],
-        )
-    )
-    loads.append(pltpu.make_async_copy(up_hbm, up_all, load_sem.at[6]))
-    for load in loads:
+    loads.append(pltpu.make_async_copy(up_hbm, up_all, load_sem.at[5]))
+    for load in loads[:3]:
         load.start()
 
     barrier = pltpu.get_barrier_semaphore()
@@ -545,7 +537,7 @@
             barrier, inc=1, device_id={"grp": lax.rem(g + step, NGRP)}, device_id_type=MESH
         )
 
-    rows = 96
+    rows = D // NSEQ
 
     def norm_one(i, carry):
         at = pl.ds(pl.multiple_of(i * rows, rows), rows)
@@ -556,10 +548,11 @@
         return carry
 
     lax.fori_loop(0, T // rows, norm_one, 0)
-    exit_win[0:64, :] = jnp.zeros((64, D), BF16)
-
-    for t in range(3):
-        loads[t].wait()
+
+    for load in loads[:3]:
+        load.wait()
+    for load in loads[3:]:
+        load.start()
     lane256 = lane_ids(256)
     q_raw = dot_nn(n1[...], win[0])
     k_raw = dot_nn(n1[...], win[1])
@@ -648,7 +641,6 @@
         masks[h, :, pair_lanes(chips)] = jnp.where(own_id <= pair_id, count, 0.0).astype(BF16)
 
     half = T // 2
-    width = part + 64
     piece = D // NSEQ
 
     def pack_half(tile, high):
@@ -695,6 +687,32 @@
         if d < NGRP - 1:
             launch(name + str(d), copies)
 
+    def weight_direct(name, at, ssem, rsem):
+        def copies():
+            found = []
+            for step in range(1, NGRP):
+                peer = lax.rem(g + step, NGRP)
+                found.append((always, to_grp(peer, at(g), at(g), ssem().at[step - 1, 0], rsem().at[g])))
+            return found
+
+        launch(name, copies)
+
+    def weight_wait(name, at, ssem, rsem):
+        for step in range(1, NGRP):
+            slot = lax.rem(g + step, NGRP)
+            to_grp(slot, at(slot), at(slot), ssem().at[0, 0], rsem().at[slot]).wait_recv()
+
+    def chain_parts(name, views, ssem, rsem):
+        return [
+            (name + str(i), view, lambda i=i: ssem.at[i], lambda i=i: rsem.at[i])
+            for i, view in enumerate(views)
+        ]
+
+    def chain_finish(parts):
+        for d in range(1, NGRP):
+            for part_of in parts:
+                chain_step(d, *part_of)
+
     def direct_start(name, at, ssem, rsem):
         def copies():
             found = []
@@ -709,6 +727,15 @@
         for step in range(1, NGRP):
             slot = lax.rem(g + step, NGRP)
             to_grp(slot, at(slot), at(slot), ssem.at[0], rsem.at[slot]).wait_recv()
+
+    loads[3].wait()
+
+    def cot_times_down(i, carry):
+        at = pl.ds(pl.multiple_of(i * T, T), T)
+        ghid[:, at] = dot_nt(cot_ref[...], down_all[at, :]).astype(BF16)
+        return carry
+
+    lax.fori_loop(0, FF // T, cot_times_down, 0)
 
     acc_a[...] = jnp.zeros_like(acc_a)
     shift[...] = jnp.zeros_like(shift)
@@ -756,8 +783,15 @@
     for h in range(3):
         tile = att_own[:, 0:128] if h == 0 else att_own[:, 128:256]
         zmix[g, h] = pack_half(tile, h != 1)
-    mixed_gather = ("mixed", lambda i: zmix.at[i], zm_ssem, zm_rsem)
-    direct_start(*mixed_gather)
+    quarter = half // 2
+    mixed_gather = chain_parts(
+        "mixed",
+        (lambda i: zmix.at[i, :, 0:quarter], lambda i: zmix.at[i, :, quarter:half]),
+        zm_ssem,
+        zm_rsem,
+    )
+    for part_of in mixed_gather:
+        chain_start(*part_of)
 
     for d in range(1, chips):
 
@@ -780,15 +814,7 @@
     launched["kv on"] = lambda: hand_on(kv, kv_ssem, kv_rsem, True)
     launched["do on"] = lambda: hand_on(dob, do_ssem, do_rsem, False)
 
-    loads[3].wait()
-
-    def cot_times_down(i, carry):
-        at = pl.ds(pl.multiple_of(i * T, T), T)
-        ghid[:, at] = dot_nt(cot_ref[...], down_all[at, :]).astype(BF16)
-        return carry
-
-    lax.fori_loop(0, FF // T, cot_times_down, 0)
-    direct_wait(*mixed_gather)
+    chain_finish(mixed_gather)
     for tile in range(D // LANES):
         (g_a, h_a), (g_b, h_b) = divmod(2 * tile, 3), divmod(2 * tile + 1, 3)
         first_head = zmix[g_a, h_a].astype(F32)
@@ -811,28 +837,62 @@
 
     lax.fori_loop(0, T // rows, norm_two, 0)
 
-    def reduce_start(i, pieces, first_in, cond=None, tag=""):
+    class Stacked:
+        def __init__(self, pieces, first_in, second_in):
+            self.pieces, self.first_in, self.second_in = pieces, first_in, second_in
+
+        def whole(self, k):
+            return self.pieces.at[k]
+
+        def block(self, k, cc):
+            return self.pieces.at[k, cc]
+
+        def first(self, cc):
+            return self.first_in.at[cc]
+
+    class Tiled(Stacked):
+        def rows(self, k):
+            count = self.first_in.shape[0]
+            return pl.ds(pl.multiple_of(count * k, count), count)
+
+        def cols(self, cc):
+            return pl.ds(pl.multiple_of(D * cc, LANES), D)
+
+        def whole(self, k):
+            return self.pieces.at[self.rows(k), :]
+
+        def block(self, k, cc):
+            return self.pieces.at[self.rows(k), self.cols(cc)]
+
+        def first(self, cc):
+            return self.first_in.at[:, self.cols(cc)]
+
+    sum_up = Stacked(pc_up, r1_up, r2_up)
+    sum_down = Tiled(up_all, r1_down, r2_down)
+    sum_eq = Stacked(pc_eq, r1_eq, r2_eq)
+    sum_ekv = Stacked(pc_ekv, r1_ekv, r2_ekv)
+    sum_exit = Tiled(ghid, r1_exit, r2_exit)
+
+    def reduce_start(i, parts):
         launch(
-            f"first{i}{tag}",
+            f"first{i}",
             lambda: [
                 (
-                    always if cond is None else cond(),
-                    to_seq(sib, pieces.at[1 - core], first_in, rs_s1.at[i], rs_r1.at[i]),
+                    always,
+                    to_seq(sib, parts.whole(1 - core), parts.first_in, rs_s1.at[i], rs_r1.at[i]),
                 )
             ],
         )
 
-    def reduce_pass(i, pieces, first_in, second_in, cond=None, tag=""):
-        def given():
-            return always if cond is None else cond()
-
-        @pl.when(given())
-        def _():
-            to_seq(sib, pieces.at[core], first_in, rs_s1.at[i], rs_r1.at[i]).wait_recv()
-            for cc in range(chips):
-                pieces[core, cc] = (
-                    pieces[core, cc].astype(F32) + first_in[cc].astype(F32)
-                ).astype(BF16)
+    def reduce_pass(i, parts):
+        to_seq(sib, parts.whole(core), parts.first_in, rs_s1.at[i], rs_r1.at[i]).wait_recv()
+
+        def add(cc, carry):
+            block = parts.block(core, cc)
+            block[...] = (block[...].astype(F32) + parts.first(cc)[...].astype(F32)).astype(BF16)
+            return carry
+
+        lax.fori_loop(0, chips, add, 0)
 
         def copies():
             found = []
@@ -840,35 +900,32 @@
                 to_chip = lax.rem(chip + d, chips)
                 copy = to_seq(
                     2 * to_chip + core,
-                    pieces.at[core, to_chip],
-                    second_in.at[chip],
+                    parts.block(core, to_chip),
+                    parts.second_in.at[chips - d - 1],
                     rs_s2.at[i, d - 1],
-                    rs_r2.at[i, chip],
+                    rs_r2.at[i, chips - d - 1],
                 )
-                found.append((given(), copy))
+                found.append((always, copy))
             return found
 
-        launch(f"second{i}{tag}", copies)
+        launch(f"second{i}", copies)
+
+    def reduce_end(i, parts):
+        result = parts.block(core, chip)[...].astype(F32)
+        for d in range(1, chips):
+            landed = parts.second_in.at[d - 1]
+            to_seq(sib, landed, landed, rs_s1.at[i], rs_r2.at[i, d - 1]).wait_recv()
+            result = result + landed[...].astype(F32)
+        return result.astype(BF16)
 
     def weight_gather(i, gathered):
         return ("weight" + str(i), lambda j: gathered.at[j], lambda: rs_zs.at[i], lambda: rs_zr.at[i])
 
-    def reduce_end(i, pieces, second_in, gathered):
-        result = pieces[core, chip].astype(F32)
-        for d in range(1, chips):
-            slot = lax.rem(chip + d, chips)
-            to_seq(
-                sib, second_in.at[slot], second_in.at[slot], rs_s1.at[i], rs_r2.at[i, slot]
-            ).wait_recv()
-            result = result + second_in[slot].astype(F32)
-        gathered[g] = result.astype(BF16)
-        chain_start(*weight_gather(i, gathered))
-
-    loads[6].wait()
-    cot_turned = jnp.transpose(
-        cot_ref[:, pl.ds(pl.multiple_of(lax.rem(g, 3) * width, LANES), width)].astype(F32)
-    ).astype(BF16)
-
+    def gather_sum(i, parts, gathered):
+        gathered[g] = reduce_end(i, parts)
+        weight_direct(*weight_gather(i, gathered))
+
+    loads[5].wait()
     def feed_forward(i, carry):
         c = lax.rem(g + i, NGRP)
         at = pl.ds(pl.multiple_of(c * D, LANES), D)
@@ -879,12 +936,6 @@
         density = jnp.exp2(hidden * hidden * (-0.5 * LOG2E)) * 0.3989422804014327
         ghid[:, at] = (ghid[:, at].astype(F32) * (cdf + hidden * density)).astype(BF16)
 
-        @pl.when(g < 3)
-        def _():
-            turned = dot_nn(cot_turned, active[:, at]).astype(BF16)
-            pc_down[0, c] = turned[:, 0:T]
-            pc_down[1, c] = turned[:, T : 2 * T]
-
         @pl.when(i == 0)
         def _():
             for j in range(2):
@@ -893,16 +944,15 @@
                     pc_up[t % 2, t // 2, :, T * j : T * j + T] = up_grad[
                         piece * t : piece * t + piece, :
                     ].astype(BF16)
-            reduce_start(0, pc_up, r1_up)
+            reduce_start(0, sum_up)
 
         @pl.when(i == 1)
         def _():
-            reduce_pass(0, pc_up, r1_up, r2_up)
+            reduce_pass(0, sum_up)
 
         return carry
 
     lax.fori_loop(0, NGRP, feed_forward, 0)
-    reduce_start(1, pc_down, r1_down, lambda: g < 3, "down")
 
     def back_through_up(i, carry):
         at = pl.ds(pl.multiple_of(i * 256, 256), 256)
@@ -910,7 +960,6 @@
         return carry
 
     lax.fori_loop(0, D // 256, back_through_up, 0)
-    reduce_pass(1, pc_down, r1_down, r2_down, lambda: g < 3, "down")
 
     stat[s] = jnp.zeros((8, D), F32)
 
@@ -928,7 +977,11 @@
             - plain * jnp.mean(scaled * plain, axis=1, keepdims=True)
         )
         grad = cot_ref[at, :].astype(F32) + inverse * inner
-        gmid[at, :] = grad
+
+        @pl.when(i == g)
+        def _():
+            gmid[...] = grad
+
         gbranch[at, :] = grad.astype(BF16)
         stat[s, 0:1, :] += jnp.sum(upstream * plain, axis=0, keepdims=True)
         stat[s, 1:2, :] += jnp.sum(upstream, axis=0, keepdims=True)
@@ -936,8 +989,10 @@
 
     lax.fori_loop(0, T // rows, norm_two_back, 0)
 
-    loads[5].wait()
-    gmix = dot_nt(gbranch[...], exit_win[...]).astype(BF16).astype(F32)
+    window = pl.ds(pl.multiple_of(jnp.maximum(part * g - 64, 0), 64), 256)
+    gmix = dot_nt(gbranch[...], exit_all[window, :])
+    gmix = jnp.where(g == 0, pltpu.roll(gmix, 64, axis=1), gmix)
+    gmix = jnp.where(lane256 < 64, 0.0, gmix).astype(BF16).astype(F32)
     numer_grad = gmix * invden[...]
     product = numer_grad * att[...]
     for h in range(3):
@@ -951,20 +1006,20 @@
 
     spread("do", dob, do_ssem, do_rsem, False)
 
-    reduce_end(0, pc_up, r2_up, ag_up)
-
-    @pl.when(g == 3)
-    def _():
-        exit_grad = dot_tn(mixed[...], gbranch[...]).astype(BF16)
+
+    def down_piece(t, carry):
+        at = pl.ds(pl.multiple_of(t * T, T), T)
+        sum_down.block(t % 2, t // 2)[...] = dot_tn(active[:, at], cot_ref[...]).astype(BF16)
+        return carry
+
+    lax.fori_loop(0, NSEQ, down_piece, 0)
+    reduce_start(1, sum_down)
+    for i in range(2):
+        exit_grad = dot_tn(mixed[...], gbranch[:, T * i : T * i + T]).astype(BF16)
         for t in range(NSEQ):
-            for i in range(2):
-                pc_down[t % 2, t // 2, piece * i : piece * i + piece, :] = exit_grad[
-                    piece * t : piece * t + piece, T * i : T * i + T
-                ]
-            pc_down[t % 2, t // 2, 2 * piece : width, :] = jnp.zeros((width - 2 * piece, T), BF16)
-
-    reduce_start(1, pc_down, r1_down, lambda: g == 3, "exit")
-    reduce_pass(1, pc_down, r1_down, r2_down, lambda: g == 3, "exit")
+            first, low = D * (t // 2) + T * i, piece * (t % 2)
+            ghid[low : low + piece, first : first + T] = exit_grad[piece * t : piece * t + piece, :]
+    reduce_start(4, sum_exit)
 
     for h in range(3):
         qmask[h] = (dob[s].astype(F32) * slot_mask(h + 1)).astype(BF16)
@@ -982,14 +1037,16 @@
 
     lax.fori_loop(0, chip + 1, query_side, 0)
     dq = acc_a[...] * scale
+    gather_sum(0, sum_up, ag_up)
 
     def weight_pieces(pieces, grad):
         for t in range(NSEQ):
             pieces[t % 2, t // 2] = grad[piece * t : piece * t + piece, :].astype(BF16)
 
     weight_pieces(pc_eq, dot_tn(n1[...], dq.astype(BF16)))
-    reduce_start(2, pc_eq, r1_eq)
-    chain_step(1, *weight_gather(0, ag_up))
+    reduce_start(2, sum_eq)
+
+    reduce_pass(4, sum_exit)
 
     v_tile = kv[s, :, 128:384].astype(F32)
     k_tile = kv[s, :, 0:256].astype(F32)
@@ -1016,12 +1073,7 @@
 
         @pl.when(j == 0)
         def _():
-            reduce_pass(2, pc_eq, r1_eq, r2_eq)
-            chain_step(2, *weight_gather(0, ag_up))
-
-        @pl.when((j == 1) | ((j == 0) & (chip == chips - 1)))
-        def _():
-            reduce_end(1, pc_down, r2_down, ag_down)
+            reduce_pass(2, sum_eq)
 
         return carry
 
@@ -1046,14 +1098,34 @@
 
     launch("rows", row_copies)
 
-    dpack = ghid.at[:, 0:384]
+    def norm_one_sums(i, carry):
+        at = pl.ds(pl.multiple_of(i * rows, rows), rows)
+        value = tok_ref[at, :].astype(F32)
+        centered = value - jnp.mean(value, axis=1, keepdims=True)
+        inverse = lax.rsqrt(jnp.mean(centered * centered, axis=1, keepdims=True) + EPS)
+        stat[s, 2:3, :] += jnp.sum(gn2[at, :] * (centered * inverse), axis=0, keepdims=True)
+        stat[s, 3:4, :] += jnp.sum(gn2[at, :], axis=0, keepdims=True)
+        return carry
+
+    lax.fori_loop(0, T // rows, norm_one_sums, 0)
+
+    def stat_copies():
+        found = []
+        for step in range(1, NSEQ):
+            peer = lax.rem(s + step, NSEQ)
+            copy = to_seq(peer, stat.at[s], stat.at[s], st_ssem.at[step - 1], st_rsem.at[s])
+            found.append((always, copy))
+        return found
+
+    launch("stat", stat_copies)
+
+    dpack = exit_all.at[0:T, 0:384]
     dpack[:, 0:128] = dk[:, 0:128].astype(BF16)
     dpack[:, 128:256] = join_halves(dk[:, 128:256], dv[:, 0:128]).astype(BF16)
     dpack[:, 256:384] = dv[:, 128:256].astype(BF16)
     weight_pieces(pc_ekv, dot_tn(n1[...], dpack[...]))
-    reduce_start(3, pc_ekv, r1_ekv)
-    chain_step(1, *weight_gather(1, ag_down))
-    reduce_end(2, pc_eq, r2_eq, ag_eq)
+    reduce_start(3, sum_ekv)
+    gather_sum(2, sum_eq, ag_eq)
 
     def through_down(i, carry):
         at = pl.ds(pl.multiple_of(i * 256, 256), 256)
@@ -1061,9 +1133,8 @@
         return carry
 
     lax.fori_loop(0, D // 256, through_down, 0)
-    reduce_pass(3, pc_ekv, r1_ekv, r2_ekv)
-    chain_step(2, *weight_gather(1, ag_down))
-    chain_step(1, *weight_gather(2, ag_eq))
+    reduce_pass(3, sum_ekv)
+    reduce_pass(1, sum_down)
 
     upstream = gn2[own_rows, :]
     for step in range(1, NGRP):
@@ -1080,23 +1151,20 @@
         - jnp.mean(scaled, axis=1, keepdims=True)
         - plain * jnp.mean(scaled * plain, axis=1, keepdims=True)
     )
-    tz[g] = (gmid[own_rows, :] + inverse * inner).astype(BF16)
-    token_gather = ("token", lambda i: tz.at[i], zt_ssem, zt_rsem)
-    direct_start(*token_gather)
-    stat[s, 2:3, :] = jnp.sum(upstream * plain, axis=0, keepdims=True)
-    stat[s, 3:4, :] = jnp.sum(upstream, axis=0, keepdims=True)
-
-    def stat_copies():
-        found = []
-        for step in range(1, NSEQ):
-            peer = lax.rem(s + step, NSEQ)
-            copy = to_seq(peer, stat.at[s], stat.at[s], st_ssem.at[step - 1], st_rsem.at[s])
-            found.append((always, copy))
-        return found
-
-    launch("stat", stat_copies)
-    reduce_end(3, pc_ekv, r2_ekv, ag_ekv)
-    chain_step(2, *weight_gather(2, ag_eq))
+    tz[g] = (gmid[...] + inverse * inner).astype(BF16)
+    middle_row = piece // 2
+    token_gather = chain_parts(
+        "token",
+        (lambda i: tz.at[i, 0:middle_row], lambda i: tz.at[i, middle_row:piece]),
+        zt_ssem,
+        zt_rsem,
+    )
+    for part_of in token_gather:
+        chain_start(*part_of)
+
+    gather_sum(3, sum_ekv, ag_ekv)
+
+    chain_finish(token_gather)
 
     for step in range(1, NSEQ):
         slot = lax.rem(s + step, NSEQ)
@@ -1107,17 +1175,13 @@
     stat_z[g] = total_stat
     direct_start("stat z", lambda i: stat_z.at[i], sz_ssem, sz_rsem)
 
-    chain_step(3, *weight_gather(0, ag_up))
-    chain_step(1, *weight_gather(3, ag_ekv))
+    weight_wait(*weight_gather(0, ag_up))
+    pass
     for i in range(NGRP):
         oup_ref[:, D * i : D * i + D] = ag_up[i]
-    chain_step(3, *weight_gather(1, ag_down))
-    chain_step(2, *weight_gather(3, ag_ekv))
-    for i in range(3):
-        odown_ref[:, width * i : width * i + width] = jnp.transpose(ag_down[i].astype(F32)).astype(BF16)
-    for i in range(2):
-        oexit_ref[:, T * i : T * i + T] = ag_down[3, piece * i : piece * i + piece, :]
-    chain_step(3, *weight_gather(2, ag_eq))
+    pass
+    oexit_ref[...] = reduce_end(4, sum_exit)
+    weight_wait(*weight_gather(2, ag_eq))
 
     def place_entry(first, tiles):
         for tile, value in enumerate(tiles):
@@ -1136,7 +1200,7 @@
                 join_halves(turned, swap_halves(b[:, 128:256])),
             ),
         )
-    direct_wait(*token_gather)
+    odown_ref[...] = reduce_end(1, sum_down)
     for i in range(NGRP):
         tgrad_ref[piece * i : piece * i + piece, :] = tz[i]
     total_stat = jnp.zeros((8, D), F32)
@@ -1147,7 +1211,7 @@
         total_stat = total_stat + stat_z[i]
     row_id = lax.broadcasted_iota(jnp.int32, (8, 1), 0)
     ostat_ref[...] = jnp.where(row_id < 2, stat_z[g], total_stat)
-    chain_step(3, *weight_gather(3, ag_ekv))
+    weight_wait(*weight_gather(3, ag_ekv))
     for pair in range(NGRP // 2):
         a = ag_ekv[2 * pair].astype(F32)
         b = ag_ekv[2 * pair + 1].astype(F32)
@@ -1272,13 +1336,12 @@
     scratch = [
         pltpu.VMEM((3, D, 256), BF16),
         pltpu.VMEM((D, D), BF16),
-        pltpu.VMEM((256, D), BF16),
         pltpu.VMEM((D, FF), BF16),
         pltpu.VMEM((FF, D), BF16),
         pltpu.VMEM((T, D), BF16),
         pltpu.VMEM((T, D), BF16),
         pltpu.VMEM((T, D), F32),
-        pltpu.VMEM((T, D), F32),
+        pltpu.VMEM((piece, D), F32),
         pltpu.VMEM((T, D), BF16),
         pltpu.VMEM((T, D), BF16),
         pltpu.VMEM((T, FF), BF16),
@@ -1302,11 +1365,17 @@
         pltpu.VMEM((NSEQ, 8, D), F32),
         pltpu.VMEM((NGRP, 8, D), F32),
     ]
-    for rows, cols in ((piece, D), (256, T), (piece, 256), (piece, 384)):
+    scratch += [
+        pltpu.VMEM((piece, chips * D), BF16),
+        pltpu.VMEM((chips - 1, piece, D), BF16),
+        pltpu.VMEM((T, chips * D), BF16),
+        pltpu.VMEM((chips - 1, T, D), BF16),
+    ]
+    for rows, cols in ((piece, D), (piece, 256), (piece, 384)):
         scratch += [
             pltpu.VMEM((2, chips, rows, cols), BF16),
             pltpu.VMEM((chips, rows, cols), BF16),
-            pltpu.VMEM((chips, rows, cols), BF16),
+            pltpu.VMEM((chips - 1, rows, cols), BF16),
             pltpu.VMEM((NGRP, rows, cols), BF16),
         ]
     scratch += [
@@ -1317,16 +1386,16 @@
         dma((NSEQ,)),
         dma((7,)),
         dma((NSEQ,)),
+        dma((2, 3, 2)),
+        dma((2, NGRP)),
         dma((NGRP - 1,)),
         dma((NGRP,)),
-        dma((NGRP - 1,)),
-        dma((NGRP,)),
-        dma((NGRP - 1,)),
-        dma((NGRP,)),
-        dma((4,)),
-        dma((4,)),
-        dma((4, 3)),
-        dma((4, chips)),
+        dma((2, 3, 2)),
+        dma((2, NGRP)),
+        dma((5,)),
+        dma((5,)),
+        dma((5, 3)),
+        dma((5, chips - 1)),
         dma((4, 3, 2)),
         dma((4, NGRP)),
         dma((NSEQ - 1,)),

time: 126 us -> 116 us (0.921)
  Pallas kernels: 124 us -> 114 us
    pallas_call x1, Pallas kernels: 121 us -> 110 us  [fast_on_device(): pl.pallas_call(partial(layer_kernel, sizes), out_shape=out_shape, in_spec...]
where the time goes in v4:
time: 116 us; the launch traced here: 115 us
  Pallas kernels  114 us (98%)
    pallas_call x1, Pallas kernels, fast_on_device(): pl.pallas_call(partial(layer_kernel, sizes), out_shape=out_shape, in_spec...  110 us
    pallas_call x1, Pallas kernels, fast_on_device(): pl.pallas_call(finish_kernel, out_shape=finish_shape, in_specs=[anywhere]...  3.95 us

profile of v4, /device:TPU:0, one launch (start us, length us, event | category | flops | bytes accessed | tf_op | source)
XLA Modules:
  0.0 114.5 jit_solution(16221304803597356271)
XLA Ops:
  0.6 109.7 %layer.1 = (bf16[384,768]{1,0:T(8,128)(2,1)}, bf16[384,768]{1,0:T(8,128)(2,1)}, bf16[96,2304]{1,0:T(8,128)(2,1)}, bf16[96,768]{1,0:T(8,128)(2,1)}, bf16[96,3072]...) custom-call(s32[4]{0:T(128)} %dil_ref.1, s32[4,12]{1,0:T(4,128)} %off_ref.1, bf16[384,768]{1,0:T(8,128)(2,1)} %tok_ref.1, ...), custom_call_target="tpu_custom_call" | custom-call | tf_op jit(solution)/shard_map/layer/pallas_call | solution.py:1415
  110.4 4.0 %finish.1 = (bf16[384,768]{1,0:T(8,128)(2,1)}, bf16[384,768]{1,0:T(8,128)(2,1)}, f32[96,2304]{1,0:T(8,128)}, f32[96,768]{1,0:T(8,128)}, f32[96,3072]{1,0:T(8,128...) custom-call(bf16[384,768]{1,0:T(8,128)(2,1)} %get-tuple-element.17.out_in, ...), custom_call_target="tpu_custom_call" | custom-call | tf_op jit(solution)/shard_map/finish/pallas_call | solution.py:1448

commit v5 on v4

--- a/solution.py
+++ b/solution.py
@@ -713,6 +713,42 @@
             for part_of in parts:
                 chain_step(d, *part_of)
 
+    def near_start(name, at, ssem, rsem):
+        def copies():
+            found = []
+            for i, step in enumerate((1, -1, 2, -2)):
+                peer = g + step
+                to = lax.rem(peer + NGRP, NGRP)
+                sem = ssem().at[i // 2, i % 2]
+                found.append(((peer >= 0) & (peer < NGRP), to_grp(to, at(g), at(g), sem, rsem().at[g])))
+            return found
+
+        launch(name, copies)
+
+    def near_forward(name, at, ssem, rsem):
+        ends = ((NGRP - 2, 0, NGRP - 1), (1, NGRP - 1, 0))
+
+        def copies():
+            return [
+                (g == near, to_grp(end, at(far), at(far), ssem().at[2, 0], rsem().at[far]))
+                for near, far, end in ends
+            ]
+
+        for near, far, end in ends:
+            pl.when(g == near)(
+                to_grp(end, at(far), at(far), ssem().at[2, 0], rsem().at[far]).wait_recv
+            )
+        launch(name + "on", copies)
+
+    def near_wait(name, at, ssem, rsem):
+        for slot in range(NGRP):
+            handed = ((g == NGRP - 2) & (slot == 0)) | ((g == 1) & (slot == NGRP - 1))
+            pl.when((g != slot) & jnp.logical_not(handed))(
+                to_grp(
+                    lax.rem(g + 1, NGRP), at(slot), at(slot), ssem().at[0, 0], rsem().at[slot]
+                ).wait_recv
+            )
+
     def direct_start(name, at, ssem, rsem):
         def copies():
             found = []
@@ -923,7 +959,8 @@
 
     def gather_sum(i, parts, gathered):
         gathered[g] = reduce_end(i, parts)
-        weight_direct(*weight_gather(i, gathered))
+        start = near_start if i in (0, 2, 3) else weight_direct
+        start(*weight_gather(i, gathered))
 
     loads[5].wait()
     def feed_forward(i, carry):
@@ -1097,6 +1134,7 @@
         return found
 
     launch("rows", row_copies)
+    near_forward(*weight_gather(0, ag_up))
 
     def norm_one_sums(i, carry):
         at = pl.ds(pl.multiple_of(i * rows, rows), rows)
@@ -1127,14 +1165,15 @@
     reduce_start(3, sum_ekv)
     gather_sum(2, sum_eq, ag_eq)
 
+    reduce_pass(3, sum_ekv)
+    reduce_pass(1, sum_down)
+
     def through_down(i, carry):
         at = pl.ds(pl.multiple_of(i * 256, 256), 256)
         out_ref[:, at] = (middle[:, at] + dot_nn(active[...], down_all[:, at])).astype(BF16)
         return carry
 
     lax.fori_loop(0, D // 256, through_down, 0)
-    reduce_pass(3, sum_ekv)
-    reduce_pass(1, sum_down)
 
     upstream = gn2[own_rows, :]
     for step in range(1, NGRP):
@@ -1163,8 +1202,10 @@
         chain_start(*part_of)
 
     gather_sum(3, sum_ekv, ag_ekv)
+    near_forward(*weight_gather(2, ag_eq))
 
     chain_finish(token_gather)
+    near_forward(*weight_gather(3, ag_ekv))
 
     for step in range(1, NSEQ):
         slot = lax.rem(s + step, NSEQ)
@@ -1175,13 +1216,13 @@
     stat_z[g] = total_stat
     direct_start("stat z", lambda i: stat_z.at[i], sz_ssem, sz_rsem)
 
-    weight_wait(*weight_gather(0, ag_up))
+    near_wait(*weight_gather(0, ag_up))
     pass
     for i in range(NGRP):
         oup_ref[:, D * i : D * i + D] = ag_up[i]
     pass
     oexit_ref[...] = reduce_end(4, sum_exit)
-    weight_wait(*weight_gather(2, ag_eq))
+    near_wait(*weight_gather(2, ag_eq))
 
     def place_entry(first, tiles):
         for tile, value in enumerate(tiles):
@@ -1211,7 +1252,7 @@
         total_stat = total_stat + stat_z[i]
     row_id = lax.broadcasted_iota(jnp.int32, (8, 1), 0)
     ostat_ref[...] = jnp.where(row_id < 2, stat_z[g], total_stat)
-    weight_wait(*weight_gather(3, ag_ekv))
+    near_wait(*weight_gather(3, ag_ekv))
     for pair in range(NGRP // 2):
         a = ag_ekv[2 * pair].astype(F32)
         b = ag_ekv[2 * pair + 1].astype(F32)

time: 116 us -> 111 us (0.957)
  Pallas kernels: 114 us -> 110 us
    pallas_call x1, Pallas kernels: 110 us -> 106 us  [fast_on_device(): pl.pallas_call(partial(layer_kernel, sizes), out_shape=out_shape, in_spec...]
where the time goes in v5:
time: 111 us
  Pallas kernels  110 us (99%)
    pallas_call x1, Pallas kernels, fast_on_device(): pl.pallas_call(partial(layer_kernel, sizes), out_shape=out_shape, in_spec...  106 us
    pallas_call x1, Pallas kernels, fast_on_device(): pl.pallas_call(finish_kernel, out_shape=finish_shape, in_specs=[anywhere]...  3.95 us

profile of v5, /device:TPU:0, one launch (start us, length us, event | category | flops | bytes accessed | tf_op | source)
XLA Modules:
  0.0 110.7 jit_solution(4312020997865459765)
XLA Ops:
  0.6 105.9 %layer.1 = (bf16[384,768]{1,0:T(8,128)(2,1)}, bf16[384,768]{1,0:T(8,128)(2,1)}, bf16[96,2304]{1,0:T(8,128)(2,1)}, bf16[96,768]{1,0:T(8,128)(2,1)}, bf16[96,3072]...) custom-call(s32[4]{0:T(128)} %dil_ref.1, s32[4,12]{1,0:T(4,128)} %off_ref.1, bf16[384,768]{1,0:T(8,128)(2,1)} %tok_ref.1, ...), custom_call_target="tpu_custom_call" | custom-call | tf_op jit(solution)/shard_map/layer/pallas_call | solution.py:1456
  106.5 4.0 %finish.1 = (bf16[384,768]{1,0:T(8,128)(2,1)}, bf16[384,768]{1,0:T(8,128)(2,1)}, f32[96,2304]{1,0:T(8,128)}, f32[96,768]{1,0:T(8,128)}, f32[96,3072]{1,0:T(8,128...) custom-call(bf16[384,768]{1,0:T(8,128)(2,1)} %get-tuple-element.17.out_in, ...), custom_call_target="tpu_custom_call" | custom-call | tf_op jit(solution)/shard_map/finish/pallas_call | solution.py:1489

commit v6 on v5

--- a/solution.py
+++ b/solution.py
@@ -687,21 +687,6 @@
         if d < NGRP - 1:
             launch(name + str(d), copies)
 
-    def weight_direct(name, at, ssem, rsem):
-        def copies():
-            found = []
-            for step in range(1, NGRP):
-                peer = lax.rem(g + step, NGRP)
-                found.append((always, to_grp(peer, at(g), at(g), ssem().at[step - 1, 0], rsem().at[g])))
-            return found
-
-        launch(name, copies)
-
-    def weight_wait(name, at, ssem, rsem):
-        for step in range(1, NGRP):
-            slot = lax.rem(g + step, NGRP)
-            to_grp(slot, at(slot), at(slot), ssem().at[0, 0], rsem().at[slot]).wait_recv()
-
     def chain_parts(name, views, ssem, rsem):
         return [
             (name + str(i), view, lambda i=i: ssem.at[i], lambda i=i: rsem.at[i])
@@ -819,10 +804,9 @@
     for h in range(3):
         tile = att_own[:, 0:128] if h == 0 else att_own[:, 128:256]
         zmix[g, h] = pack_half(tile, h != 1)
-    quarter = half // 2
     mixed_gather = chain_parts(
         "mixed",
-        (lambda i: zmix.at[i, :, 0:quarter], lambda i: zmix.at[i, :, quarter:half]),
+        [lambda i, n=n: zmix.at[i, :, n * half // 3 : (n + 1) * half // 3] for n in range(3)],
         zm_ssem,
         zm_rsem,
     )
@@ -959,8 +943,7 @@
 
     def gather_sum(i, parts, gathered):
         gathered[g] = reduce_end(i, parts)
-        start = near_start if i in (0, 2, 3) else weight_direct
-        start(*weight_gather(i, gathered))
+        near_start(*weight_gather(i, gathered))
 
     loads[5].wait()
     def feed_forward(i, carry):
@@ -1134,7 +1117,6 @@
         return found
 
     launch("rows", row_copies)
-    near_forward(*weight_gather(0, ag_up))
 
     def norm_one_sums(i, carry):
         at = pl.ds(pl.multiple_of(i * rows, rows), rows)
@@ -1166,6 +1148,7 @@
     gather_sum(2, sum_eq, ag_eq)
 
     reduce_pass(3, sum_ekv)
+    near_forward(*weight_gather(0, ag_up))
     reduce_pass(1, sum_down)
 
     def through_down(i, carry):
@@ -1427,8 +1410,8 @@
         dma((NSEQ,)),
         dma((7,)),
         dma((NSEQ,)),
-        dma((2, 3, 2)),
-        dma((2, NGRP)),
+        dma((3, 3, 2)),
+        dma((3, NGRP)),
         dma((NGRP - 1,)),
         dma((NGRP,)),
         dma((2, 3, 2)),

time: 111 us -> 110 us (level)
  no operation moved by 1% of the time
where the time goes in v6:
time: 110 us
  Pallas kernels  109 us (99%)
    pallas_call x1, Pallas kernels, fast_on_device(): pl.pallas_call(partial(layer_kernel, sizes), out_shape=out_shape, in_spec...  105 us
    pallas_call x1, Pallas kernels, fast_on_device(): pl.pallas_call(finish_kernel, out_shape=finish_shape, in_specs=[anywhere]...  3.95 us

profile of v6, /device:TPU:0, one launch (start us, length us, event | category | flops | bytes accessed | tf_op | source)
XLA Modules:
  0.0 110.1 jit_solution(12421001292321579716)
XLA Ops:
  0.6 105.4 %layer.1 = (bf16[384,768]{1,0:T(8,128)(2,1)}, bf16[384,768]{1,0:T(8,128)(2,1)}, bf16[96,2304]{1,0:T(8,128)(2,1)}, bf16[96,768]{1,0:T(8,128)(2,1)}, bf16[96,3072]...) custom-call(s32[4]{0:T(128)} %dil_ref.1, s32[4,12]{1,0:T(4,128)} %off_ref.1, bf16[384,768]{1,0:T(8,128)(2,1)} %tok_ref.1, ...), custom_call_target="tpu_custom_call" | custom-call | tf_op jit(solution)/shard_map/layer/pallas_call | solution.py:1439
  106.0 4.0 %finish.1 = (bf16[384,768]{1,0:T(8,128)(2,1)}, bf16[384,768]{1,0:T(8,128)(2,1)}, f32[96,2304]{1,0:T(8,128)}, f32[96,768]{1,0:T(8,128)}, f32[96,3072]{1,0:T(8,128...) custom-call(bf16[384,768]{1,0:T(8,128)(2,1)} %get-tuple-element.17.out_in, ...), custom_call_target="tpu_custom_call" | custom-call | tf_op jit(solution)/shard_map/finish/pallas_call | solution.py:1472

commit v7 on v6

--- a/solution.py
+++ b/solution.py
@@ -813,27 +813,6 @@
     for part_of in mixed_gather:
         chain_start(*part_of)
 
-    for d in range(1, chips):
-
-        @pl.when(chip + d < chips)
-        def _(d=d):
-            slot = lax.rem(s + 2 * d, NSEQ)
-            to_seq(sib, qb.at[slot], qb.at[slot], q_ssem.at[0], q_rsem.at[slot]).wait_recv()
-
-    def hand_on(buffer, ssem, rsem, upward):
-        found = []
-        for d in range(1, chips):
-            slot = lax.rem(s + (NSEQ - 2 * d if upward else 2 * d), NSEQ)
-            cond = chip >= d if upward else chip + d < chips
-            found.append(
-                (cond, to_seq(sib, buffer.at[slot], buffer.at[slot], ssem.at[3 + d], rsem.at[slot]))
-            )
-        return found
-
-    launch("q on", lambda: hand_on(qb, q_ssem, q_rsem, False))
-    launched["kv on"] = lambda: hand_on(kv, kv_ssem, kv_rsem, True)
-    launched["do on"] = lambda: hand_on(dob, do_ssem, do_rsem, False)
-
     chain_finish(mixed_gather)
     for tile in range(D // LANES):
         (g_a, h_a), (g_b, h_b) = divmod(2 * tile, 3), divmod(2 * tile + 1, 3)
@@ -945,6 +924,27 @@
         gathered[g] = reduce_end(i, parts)
         near_start(*weight_gather(i, gathered))
 
+    for d in range(1, chips):
+
+        @pl.when(chip + d < chips)
+        def _(d=d):
+            slot = lax.rem(s + 2 * d, NSEQ)
+            to_seq(sib, qb.at[slot], qb.at[slot], q_ssem.at[0], q_rsem.at[slot]).wait_recv()
+
+    def hand_on(buffer, ssem, rsem, upward):
+        found = []
+        for d in range(1, chips):
+            slot = lax.rem(s + (NSEQ - 2 * d if upward else 2 * d), NSEQ)
+            cond = chip >= d if upward else chip + d < chips
+            found.append(
+                (cond, to_seq(sib, buffer.at[slot], buffer.at[slot], ssem.at[3 + d], rsem.at[slot]))
+            )
+        return found
+
+    launch("q on", lambda: hand_on(qb, q_ssem, q_rsem, False))
+    launched["kv on"] = lambda: hand_on(kv, kv_ssem, kv_rsem, True)
+    launched["do on"] = lambda: hand_on(dob, do_ssem, do_rsem, False)
+
     loads[5].wait()
     def feed_forward(i, carry):
         c = lax.rem(g + i, NGRP)
@@ -966,7 +966,7 @@
                     ].astype(BF16)
             reduce_start(0, sum_up)
 
-        @pl.when(i == 1)
+        @pl.when(i == 2)
         def _():
             reduce_pass(0, sum_up)
 

time: 110 us -> 110 us (level)
  no operation moved by 1% of the time
where the time goes in v7:
time: 110 us; the launch traced here: 109 us
  Pallas kernels  109 us (99%)
    pallas_call x1, Pallas kernels, fast_on_device(): pl.pallas_call(partial(layer_kernel, sizes), out_shape=out_shape, in_spec...  105 us
    pallas_call x1, Pallas kernels, fast_on_device(): pl.pallas_call(finish_kernel, out_shape=finish_shape, in_specs=[anywhere]...  3.95 us

profile of v7, /device:TPU:0, one launch (start us, length us, event | category | flops | bytes accessed | tf_op | source)
XLA Modules:
  0.0 109.5 jit_solution(6597197504834042088)
XLA Ops:
  0.6 104.7 %layer.1 = (bf16[384,768]{1,0:T(8,128)(2,1)}, bf16[384,768]{1,0:T(8,128)(2,1)}, bf16[96,2304]{1,0:T(8,128)(2,1)}, bf16[96,768]{1,0:T(8,128)(2,1)}, bf16[96,3072]...) custom-call(s32[4]{0:T(128)} %dil_ref.1, s32[4,12]{1,0:T(4,128)} %off_ref.1, bf16[384,768]{1,0:T(8,128)(2,1)} %tok_ref.1, ...), custom_call_target="tpu_custom_call" | custom-call | tf_op jit(solution)/shard_map/layer/pallas_call | solution.py:1439
  105.4 4.0 %finish.1 = (bf16[384,768]{1,0:T(8,128)(2,1)}, bf16[384,768]{1,0:T(8,128)(2,1)}, f32[96,2304]{1,0:T(8,128)}, f32[96,768]{1,0:T(8,128)}, f32[96,3072]{1,0:T(8,128...) custom-call(bf16[384,768]{1,0:T(8,128)(2,1)} %get-tuple-element.17.out_in, ...), custom_call_target="tpu_custom_call" | custom-call | tf_op jit(solution)/shard_map/finish/pallas_call | solution.py:1472
